TPU v7x, 32 devices: a whole 2x2x4 slice. The times are simulated.
32 devices in a mesh: outer: 4 (over y, x), inner: 8 (over z, core).
Axes of the slice: x: 2, y: 2, z: 4, core: 2. Of those that a mesh axis runs over, the one named last changes fastest.
Arguments:
- weights: float32 [16384, 128], P(('outer', 'inner')), may hold values from -1.5 to 1.5
Outputs:
- level_weights: float32 [16384, 128], P(('outer', 'inner'))
All inputs are finite; a program needn't handle non-finite values.
Results may differ from a plain program's by a relative error of at most 0.0049.
Values sent between devices are 32-bit elements; how exact they have to be, the bound alone decides.
No kernel may reach another device: no remote copies, remote signals or barrier semaphores. Data moves between devices by JAX's collectives and lax.ppermute only.
A program may use at most 64 MiB of HBM per device.

v0:
```python
import jax
import jax.numpy as jnp
import numpy as np
from jax import lax
from jax.sharding import PartitionSpec as P

GRID_N = 16384
TREE_LEVELS = 11


def from_partner(block, axis, bit):
    count = lax.axis_size(axis)
    route = []
    for low in range(count):
        high = low | 1 << bit
        if high != low and high < count:
            route += [(low, high), (high, low)]
    return lax.ppermute(block, axis, route)


def chebyshev_nodes():
    return 0.5 * np.cos(np.pi * (2.0 * np.arange(8) + 1.0) / 16.0)


def lagrange_weights(which_child):
    node_values = chebyshev_nodes()
    targets = (node_values + which_child - 0.5) / 2.0
    weights_table = np.ones((8, 8))
    for anchor in range(8):
        for other_node in range(8):
            if other_node != anchor:
                weights_table[anchor, :] = (
                    weights_table[anchor, :]
                    * (targets - node_values[other_node])
                    / (node_values[anchor] - node_values[other_node])
                )
    return weights_table


def merge_matrix(dimension):
    merge_table = np.zeros((256, 128))
    for which_child in range(2):
        weights_table = lagrange_weights(which_child)
        if dimension == 0:
            block_table = np.kron(weights_table, np.eye(8))
        else:
            block_table = np.kron(np.eye(8), weights_table)
        for component in range(2):
            merge_table[
                which_child * 128 + component * 64 : which_child * 128 + component * 64 + 64,
                component * 64 : component * 64 + 64,
            ] = block_table.T
    return jnp.asarray(merge_table, dtype=jnp.float32)


def level_plan(local_bits, inner_bits, outer_bits):
    levels_total = inner_bits + outer_bits
    source_bits = [[], []]
    for level_number in range(levels_total):
        source_bits[(level_number + 1) % 2].append(local_bits + level_number)
    source_bits[0] = source_bits[0] + [local_bits - 7, local_bits - 6, local_bits - 5]
    source_bits[1] = source_bits[1] + [
        local_bits - 4,
        local_bits - 3,
        local_bits - 2,
        local_bits - 1,
    ]
    target_bits = [[], []]
    for ordinal in range(local_bits - 7):
        target_bits[ordinal % 2].append(ordinal)
    level_list = []
    for level_number in range(levels_total):
        dimension = (level_number + 1) % 2
        carried_bit = local_bits + level_number
        if level_number < inner_bits:
            moved_bit = local_bits - inner_bits + level_number
        else:
            moved_bit = local_bits - levels_total + level_number - inner_bits
        level_list.append(
            (
                dimension,
                carried_bit,
                moved_bit,
                [list(bit_group) for bit_group in target_bits],
                [list(bit_group) for bit_group in source_bits],
            )
        )
        target_bits = [
            [carried_bit if bit_place == moved_bit else bit_place for bit_place in bit_group]
            for bit_group in target_bits
        ]
        source_bits = [
            [carried_bit if bit_place == moved_bit else bit_place for bit_place in bit_group]
            for bit_group in source_bits
        ]
        source_bits[dimension] = source_bits[dimension][1:]
        target_bits[dimension] = [moved_bit] + target_bits[dimension]
    return level_list


def bit_value(row_index, positions):
    assembled = jnp.zeros_like(row_index)
    for ordinal, position in enumerate(positions):
        assembled = assembled + ((row_index >> position & 1) << ordinal)
    return assembled


def spread_grid(values, axis_place):
    row_count = values.shape[0]
    if axis_place == 0:
        shaped = values[:, None, :, None]
    else:
        shaped = values[:, None, None, :]
    return jnp.broadcast_to(shaped, (row_count, 2, 8, 8)).reshape(row_count, 128)


def dimension_terms(target_index, target_level, source_index, source_level):
    node_values = jnp.asarray(chebyshev_nodes(), dtype=jnp.float32)
    box_width = 2.0 ** (-source_level)
    center = (target_index.astype(jnp.float32) + 0.5) * (
        GRID_N * 2.0 ** (-target_level)
    ) - GRID_N / 2.0
    offsets = node_values * box_width
    position = (source_index.astype(jnp.float32) + 0.5)[:, None] * box_width + offsets[None, :]
    linear = offsets[None, :] * center[:, None]
    return (center, position, linear)


def phase_cycles(target_index, target_level, source_index, source_level):
    center_one, place_one, linear_one = dimension_terms(
        target_index[0], target_level[0], source_index[0], source_level[0]
    )
    center_two, place_two, linear_two = dimension_terms(
        target_index[1], target_level[1], source_index[1], source_level[1]
    )
    turn = 2.0 * np.pi
    sine_one = spread_grid(jnp.sin(turn * place_one), 0)
    sine_two = spread_grid(jnp.sin(turn * place_two), 1)
    cosine_one = spread_grid(jnp.cos(turn * place_one), 0)
    cosine_two = spread_grid(jnp.cos(turn * place_two), 1)
    coeff_one = (2.0 + sine_one * sine_two) / 16.0
    coeff_two = (2.0 + cosine_one * cosine_two) / 16.0
    radial = jnp.sqrt(
        (coeff_one * center_one[:, None]) ** 2 + (coeff_two * center_two[:, None]) ** 2
    )
    linear = spread_grid(linear_one, 0) + spread_grid(linear_two, 1)
    return linear - jnp.floor(linear) + (radial - jnp.floor(radial))


def rotate(values, cycles, direction):
    radians = 2.0 * np.pi * cycles
    cosine = jnp.cos(radians)
    sine_part = jnp.sin(radians) * direction
    swapped = jnp.concatenate([values[:, 64:], values[:, :64]], axis=1)
    sign_pattern = jnp.concatenate([-jnp.ones((64,), jnp.float32), jnp.ones((64,), jnp.float32)])
    return values * cosine + swapped * (sine_part * sign_pattern)


def combine(first_child, second_child, base_index, layout, merge_table):
    dimension, target_bits, source_bits = (layout[0], layout[3], layout[4])
    children = [first_child, second_child]
    target_index = [bit_value(base_index, target_bits[0]), bit_value(base_index, target_bits[1])]
    source_index = [bit_value(base_index, source_bits[0]), bit_value(base_index, source_bits[1])]
    source_level = [len(source_bits[0]), len(source_bits[1])]
    target_level = [TREE_LEVELS - source_level[0], TREE_LEVELS - source_level[1]]
    results = []
    for branch in range(2):
        new_target = list(target_index)
        new_target[dimension] = 2 * target_index[dimension] + branch
        new_level = list(target_level)
        new_level[dimension] = target_level[dimension] + 1
        rotated = []
        for which_child in range(2):
            child_source = list(source_index)
            child_source[dimension] = source_index[dimension] + which_child
            rotated.append(
                rotate(
                    children[which_child],
                    phase_cycles(new_target, new_level, child_source, source_level),
                    1.0,
                )
            )
        stacked = jnp.concatenate(rotated, axis=1)
        merged = jnp.dot(
            stacked,
            merge_table,
            precision=lax.Precision.HIGHEST,
            preferred_element_type=jnp.float32,
        )
        parent_source = list(source_index)
        parent_source[dimension] = source_index[dimension] // 2
        parent_level = list(source_level)
        parent_level[dimension] = source_level[dimension] - 1
        results.append(
            rotate(merged, phase_cycles(new_target, new_level, parent_source, parent_level), -1.0)
        )
    return results


def split_pairs(current, layout, global_index, own_bit):
    carried_bit, moved_bit = (layout[1], layout[2])
    row_count = current.shape[0]
    low_span = 1 << moved_bit
    high_count = row_count // (2 * low_span)
    shaped = current.reshape(high_count, 2, low_span, 128)
    indices = global_index.reshape(high_count, 2, low_span)
    chosen = own_bit == 1
    kept_half = jnp.where(chosen, shaped[:, 1], shaped[:, 0]).reshape(-1, 128)
    sent_half = jnp.where(chosen, shaped[:, 0], shaped[:, 1]).reshape(-1, 128)
    kept_index = jnp.where(chosen, indices[:, 1], indices[:, 0]).reshape(-1)
    base_index = kept_index - (kept_index >> carried_bit & 1) * (1 << carried_bit)
    return (kept_half, sent_half, base_index)


def join_pairs(kept_half, received, base_index, layout, own_bit):
    moved_bit = layout[2]
    chosen = own_bit == 1
    first_child = jnp.where(chosen, received, kept_half)
    second_child = jnp.where(chosen, kept_half, received)
    outputs = combine(first_child, second_child, base_index, layout, merge_matrix(layout[0]))
    low_span = 1 << moved_bit
    high_count = kept_half.shape[0] // low_span
    stacked = jnp.stack(
        [branch_out.reshape(high_count, low_span, 128) for branch_out in outputs], axis=1
    )
    return stacked.reshape(2 * kept_half.shape[0], 128)


def body(weights):
    row_count = weights.shape[0]
    local_bits = row_count.bit_length() - 1
    inner_size = lax.axis_size("inner")
    outer_size = lax.axis_size("outer")
    inner_bits = inner_size.bit_length() - 1
    outer_bits = outer_size.bit_length() - 1
    level_list = level_plan(local_bits, inner_bits, outer_bits)
    inner_place = lax.axis_index("inner")
    outer_place = lax.axis_index("outer")
    device_flat = outer_place * inner_size + inner_place
    global_index = device_flat * row_count + jnp.arange(row_count, dtype=jnp.int32)
    current = weights
    for level_number in range(inner_bits):
        layout = level_list[level_number]
        own_bit = inner_place >> level_number & 1
        kept_half, sent_half, base_index = split_pairs(current, layout, global_index, own_bit)
        received = from_partner(sent_half, "inner", level_number)
        current = join_pairs(kept_half, received, base_index, layout, own_bit)
    levels_total = inner_bits + outer_bits
    for level_number in range(inner_bits, levels_total):
        layout = level_list[level_number]
        own_bit = outer_place >> level_number - inner_bits & 1
        kept_half, sent_half, base_index = split_pairs(current, layout, global_index, own_bit)
        received = from_partner(sent_half, "outer", level_number - inner_bits)
        current = join_pairs(kept_half, received, base_index, layout, own_bit)
    return current


def solution(mesh):
    in_specs = (P(("outer", "inner"), None),)
    out_specs = P(("outer", "inner"), None)
    return jax.shard_map(body, mesh=mesh, in_specs=in_specs, out_specs=out_specs, check_vma=False)
```

profile of v0, /device:TPU:0, one launch (start us, length us, event | category | flops | bytes accessed | tf_op | source)
XLA Modules:
  0.0 74.2 jit_solution(14750623800466275489)
XLA Ops:
  0.0 1.0 %slice_select_fusion.8 = (f32[4,1,64,128]{3,2,1,0:T(8,128)S(1)}, f32[4,1,64,128]{3,2,1,0:T(8,128)S(1)}) fusion(f32[4,2,64,128]{3,2,1,0:T(8,128)} %bitcast.598, pred[]{:T(512)S(6)} %eq.24), kind=kLoop, calls=%fused_computation.478 | loop fusion | flops 65536 | bytes 524289 | tf_op jit(solution)/shard_map/jit(_where)/select_n | solution.py:209
  5.7 0.8 %fusion.358 = (f32[256,8]{0,1:T(8,128)S(1)}, f32[256,8]{0,1:T(8,128)S(1)}, f32[256,8]{0,1:T(8,128)S(1)}, f32[256,8]{0,1:T(8,128)S(1)}, f32[256,8]{0,1:T(8,128)S(...) fusion(f32[256]{0:T(256)S(1)} %get-tuple-element.281, ...), kind=kLoop, calls=%fused_computation.577 | loop fusion | flops 24576 | bytes 105504 | tf_op jit(solution)/shard_map/cos | solution.py:139
  7.2 0.8 %broadcast_multiply_fusion.15 = (f32[256,8]{0,1:T(8,128)S(1)}, f32[256,8]{0,1:T(8,128)S(1)}, f32[256,8]{0,1:T(8,128)S(1)}, f32[256,8]{0,1:T(8,128)}, f32[256,8]{...) fusion(f32[256]{0:T(256)S(1)} %get-tuple-element.389, ...), kind=kLoop, calls=%fused_computation.608 | loop fusion | flops 59392 | bytes 253056 | tf_op jit(solution)/shard_map/mul | solution.py:125
  8.7 0.9 %fusion.336 = (f32[256,8]{0,1:T(8,128)S(1)}, f32[256,8]{0,1:T(8,128)S(1)}, f32[256,8]{0,1:T(8,128)S(1)}, f32[256,8]{0,1:T(8,128)S(1)}, f32[256,8]{0,1:T(8,128)S(...) fusion(f32[256]{0:T(256)S(1)} %get-tuple-element.306, ...), kind=kLoop, calls=%fused_computation.544 | loop fusion | flops 40960 | bytes 175168 | tf_op jit(solution)/shard_map/cos | solution.py:139
  15.7 0.9 %broadcast_select_fusion.1 = (f32[256,128]{0,1:T(8,128)S(1)}, f32[256,128]{0,1:T(8,128)S(1)}) fusion(f32[256,128]{0,1:T(8,128)} %collective-permute-done, f32[256,128]{0,1:T(8,128)S(1)} %copy.95, pred[]{:T(512)S(6)} %eq.24), kind=kLoop, calls=%fused_computation.520 | loop fusion | flops 65536 | bytes 524289 | tf_op jit(solution)/shard_map/jit(_where)/select_n | solution.py:218
  16.7 0.8 %copy-done.1 = f32[128,128]{1,0:T(8,128)S(1)} copy-done((f32[128,128]{1,0:T(8,128)S(1)}, f32[128,128]{1,0:T(8,128)}, u32[]{:S(2)}) %copy-start.1) | copy-done | bytes 65560
  17.5 0.8 %fusion.281 = f32[256,128]{0,1:T(8,128)S(1)} fusion(f32[128,128]{1,0:T(8,128)S(1)} %copy-done.1, f32[256,128]{0,1:T(8,128)S(1)} %get-tuple-element.78, f32[256,128]{0,1:T(8,128)S(1)} %get-tuple-element.94, f32[256,64]{0,1:T(8,128)S(1)} %get-tuple-element.397, f32[256,64]{0,1:T(8,128)S(1)} %get-tuple-element.398, f32[128]{0:T(128)S(1)} %copy-done.11), kind=kOutput, calls=%fused_computation.438 | convolution fusion | flops 50495488 | bytes 590336 | tf_op jit(solution)/shard_map/dot_general | solution.py:184
  19.1 0.8 %fusion.294 = f32[256,128]{0,1:T(8,128)S(1)} fusion(f32[128,128]{1,0:T(8,128)S(1)} %copy-done.1, f32[256,128]{0,1:T(8,128)S(1)} %get-tuple-element.77, f32[256,128]{0,1:T(8,128)S(1)} %get-tuple-element.94, f32[256,64]{0,1:T(8,128)S(1)} %get-tuple-element.397, f32[256,64]{0,1:T(8,128)S(1)} %get-tuple-element.398, f32[128]{0:T(128)S(1)} %copy-done.11), kind=kOutput, calls=%fused_computation.453 | convolution fusion | flops 50495488 | bytes 590336 | tf_op jit(solution)/shard_map/dot_general | solution.py:184
  19.9 0.8 %convolution_add_fusion.9 = f32[256,128]{0,1:T(8,128)S(1)} fusion(f32[256,128]{0,1:T(8,128)S(1)} %fusion.294, f32[128,128]{1,0:T(8,128)S(1)} %copy-done, f32[256,128]{0,1:T(8,128)S(1)} %get-tuple-element.80, f32[256,128]{0,1:T(8,128)S(1)} %get-tuple-element.93, f32[256,64]{0,1:T(8,128)S(1)} %get-tuple-element.134, f32[256,64]{0,1:T(8,128)S(1)} %get-tuple-element.133, ...), kind=kOutput, calls=%fused_computation.9 | convolution fusion | flops 50528256 | bytes 721408 | tf_op jit(solution)/shard_map/dot_general | solution.py:184
  21.4 1.5 %fusion.60 = (f32[256,128]{0,1:T(8,128)S(1)}, f32[256,128]{0,1:T(8,128)S(1)}) fusion(f32[256,64]{0,1:T(8,128)S(1)} %get-tuple-element.130, f32[256,64]{0,1:T(8,128)S(1)} %get-tuple-element.129, f32[256,128]{0,1:T(8,128)S(1)} %convolution_add_fusion.9, f32[256,2,8,8]{0,3,2,1:T(8,128)S(1)} %get-tuple-element.184, f32[256,2,8,8]{0,3,2,1:T(8,128)S(1)} %get-tuple-element.177, ...), kind=kLoop, calls=%fused_computation.128 | loop fusion | flops 983040 | bytes 1314304 | tf_op jit(solution)/shard_map/add | solution.py:156
  23.3 2.6 %collective-permute-start.1 = (f32[256,128]{0,1:T(8,128)S(1)}, f32[256,128]{0,1:T(8,128)S(1)}, u32[]{:S(2)}, u32[]{:S(2)}) collective-permute-start(f32[256,128]{0,1:T(8,128)S(1)} %copy.117), channel_id=1, source_target_pairs={{0,2},{2,0},{1,3},{3,1},{4,6},{6,4},{5,7},{7,5},{8,10},{10,8},{9,1... | collective-permute-start | bytes 393224 | tf_op jit(solution)/shard_map/ppermute | solution.py:18
  26.1 4.0 %collective-permute-done.1 = f32[256,128]{0,1:T(8,128)S(1)} collective-permute-done((f32[256,128]{0,1:T(8,128)S(1)}, f32[256,128]{0,1:T(8,128)S(1)}, u32[]{:S(2)}, u32[]{:S(2)}) %collective-permute-start.1) | collective-permute-done | bytes 131104 | tf_op jit(solution)/shard_map/ppermute | solution.py:18
  30.2 0.8 %copy-done.3 = f32[128,128]{1,0:T(8,128)S(1)} copy-done((f32[128,128]{1,0:T(8,128)S(1)}, f32[128,128]{1,0:T(8,128)}, u32[]{:S(2)}) %copy-start.3) | copy-done | bytes 65560
  32.7 0.8 %fusion.268 = f32[256,128]{0,1:T(8,128)S(1)} fusion(f32[128,128]{1,0:T(8,128)S(1)} %copy-done.3, f32[256,128]{0,1:T(8,128)S(1)} %get-tuple-element.71, f32[256,128]{0,1:T(8,128)S(1)} %get-tuple-element.90, f32[256,64]{0,1:T(8,128)S(1)} %get-tuple-element.128, f32[256,64]{0,1:T(8,128)S(1)} %get-tuple-element.127, f32[128]{0:T(128)S(1)} %copy-done.11), kind=kOutput, calls=%fused_computation.421 | convolution fusion | flops 50495488 | bytes 590336 | tf_op jit(solution)/shard_map/dot_general | solution.py:184
  34.3 0.8 %copy-done.4 = f32[256,2,8,8]{0,3,2,1:T(8,128)S(1)} copy-done((f32[256,2,8,8]{0,3,2,1:T(8,128)S(1)}, f32[256,2,8,8]{0,3,2,1:T(8,128)}, u32[]{:S(2)}) %copy-start.4) | copy-done | bytes 131096
  35.2 1.3 %fusion.62 = (f32[256,128]{0,1:T(8,128)S(1)}, f32[256,128]{0,1:T(8,128)S(1)}) fusion(f32[256,64]{0,1:T(8,128)S(1)} %get-tuple-element.122, f32[256,64]{0,1:T(8,128)S(1)} %get-tuple-element.121, f32[256,128]{0,1:T(8,128)S(1)} %convolution_add_fusion.7, f32[256,2,8,8]{0,3,2,1:T(8,128)S(1)} %copy-done.10, f32[256,2,8,8]{0,3,2,1:T(8,128)S(1)} %get-tuple-element.167, ...), kind=kLoop, calls=%fused_computation.134 | loop fusion | flops 983040 | bytes 1314304 | tf_op jit(solution)/shard_map/add | solution.py:156
  37.5 2.8 %collective-permute-start.2 = (f32[256,128]{0,1:T(8,128)S(1)}, f32[256,128]{0,1:T(8,128)S(1)}, u32[]{:S(2)}, u32[]{:S(2)}) collective-permute-start(f32[256,128]{0,1:T(8,128)S(1)} %select_bitcast_fusion), channel_id=1, source_target_pairs={{0,4},{4,0},{1,5},{5,1},{2,6},{6,2},{3,7},{7,3},{8,12},{12,8},{9,1... | collective-permute-start | bytes 393224 | tf_op jit(solution)/shard_map/ppermute | solution.py:18
  40.4 6.2 %collective-permute-done.2 = f32[256,128]{0,1:T(8,128)S(1)} collective-permute-done((f32[256,128]{0,1:T(8,128)S(1)}, f32[256,128]{0,1:T(8,128)S(1)}, u32[]{:S(2)}, u32[]{:S(2)}) %collective-permute-start.2) | collective-permute-done | bytes 131104 | tf_op jit(solution)/shard_map/ppermute | solution.py:18
  46.7 0.8 %fusion.229 = f32[256,128]{0,1:T(8,128)S(1)} fusion(f32[128,128]{1,0:T(8,128)S(1)} %copy-done.1, f32[256,128]{0,1:T(8,128)S(1)} %get-tuple-element.66, f32[256,128]{0,1:T(8,128)S(1)} %get-tuple-element.40, f32[256,64]{0,1:T(8,128)S(1)} %get-tuple-element.120, f32[256,64]{0,1:T(8,128)S(1)} %get-tuple-element.119, f32[128]{0:T(128)S(1)} %copy-done.11), kind=kOutput, calls=%fused_computation.373 | convolution fusion | flops 50495488 | bytes 590336 | tf_op jit(solution)/shard_map/dot_general | solution.py:184
  48.3 0.8 %fusion.242 = f32[256,128]{0,1:T(8,128)S(1)} fusion(f32[128,128]{1,0:T(8,128)S(1)} %copy-done.1, f32[256,128]{0,1:T(8,128)S(1)} %get-tuple-element.65, f32[256,128]{0,1:T(8,128)S(1)} %get-tuple-element.40, f32[256,64]{0,1:T(8,128)S(1)} %get-tuple-element.120, f32[256,64]{0,1:T(8,128)S(1)} %get-tuple-element.119, f32[128]{0:T(128)S(1)} %copy-done.11), kind=kOutput, calls=%fused_computation.388 | convolution fusion | flops 50495488 | bytes 590336 | tf_op jit(solution)/shard_map/dot_general | solution.py:184
  49.9 0.8 %copy-done.7 = f32[256,2,8,8]{0,3,2,1:T(8,128)S(1)} copy-done((f32[256,2,8,8]{0,3,2,1:T(8,128)S(1)}, f32[256,2,8,8]{0,3,2,1:T(8,128)}, u32[]{:S(2)}) %copy-start.7) | copy-done | bytes 131096
  50.8 1.6 %fusion.65 = (f32[1,1,256,128]{2,3,1,0:T(8,128)S(1)}, f32[1,1,256,128]{2,3,1,0:T(8,128)S(1)}) fusion(f32[256,64]{0,1:T(8,128)S(1)} %get-tuple-element.114, f32[256,64]{0,1:T(8,128)S(1)} %get-tuple-element.113, f32[256,128]{0,1:T(8,128)S(1)} %convolution_add_fusion.5, f32[256,2,8,8]{0,3,2,1:T(8,128)S(1)} %copy-done.8, ...), kind=kLoop, calls=%fused_computation.141 | loop fusion | flops 983040 | bytes 1314304 | tf_op jit(solution)/shard_map/stack;reshape | solution.py:223
  52.7 1.5 %collective-permute-start.3 = (f32[256,128]{0,1:T(8,128)S(1)}, f32[256,128]{0,1:T(8,128)S(1)}, u32[]{:S(2)}, u32[]{:S(2)}) collective-permute-start(f32[256,128]{0,1:T(8,128)S(1)} %copy.105), channel_id=1, source_target_pairs={{0,8},{8,0},{16,24},{24,16},{1,9},{9,1},{17,25},{25,17},{2,10},{10... | collective-permute-start | bytes 393224 | tf_op jit(solution)/shard_map/ppermute | solution.py:18
  54.4 3.4 %collective-permute-done.3 = f32[256,128]{0,1:T(8,128)S(1)} collective-permute-done((f32[256,128]{0,1:T(8,128)S(1)}, f32[256,128]{0,1:T(8,128)S(1)}, u32[]{:S(2)}, u32[]{:S(2)}) %collective-permute-start.3) | collective-permute-done | bytes 131104 | tf_op jit(solution)/shard_map/ppermute | solution.py:18
  58.6 0.8 %convolution_add_fusion.2 = f32[256,128]{0,1:T(8,128)S(1)} fusion(f32[256,128]{0,1:T(8,128)S(1)} %fusion.203, f32[128,128]{1,0:T(8,128)S(1)} %copy-done.2, f32[256,128]{0,1:T(8,128)S(1)} %get-tuple-element.61, f32[256,128]{0,1:T(8,128)S(1)} %get-tuple-element.85, f32[256,64]{0,1:T(8,128)S(1)} %get-tuple-element.110, f32[256,64]{0,1:T(8,128)S(1)} %get-tuple-element.109, ...), kind=kOutput, calls=%fused_computation.2 | convolution fusion | flops 50528256 | bytes 721408 | tf_op jit(solution)/shard_map/dot_general | solution.py:184
  60.2 0.8 %convolution_add_fusion.3 = f32[256,128]{0,1:T(8,128)S(1)} fusion(f32[256,128]{0,1:T(8,128)S(1)} %fusion.216, f32[128,128]{1,0:T(8,128)S(1)} %copy-done.2, f32[256,128]{0,1:T(8,128)S(1)} %get-tuple-element.62, f32[256,128]{0,1:T(8,128)S(1)} %get-tuple-element.85, f32[256,64]{0,1:T(8,128)S(1)} %get-tuple-element.110, f32[256,64]{0,1:T(8,128)S(1)} %get-tuple-element.109, ...), kind=kOutput, calls=%fused_computation.3 | convolution fusion | flops 50528256 | bytes 721408 | tf_op jit(solution)/shard_map/dot_general | solution.py:184
  61.0 0.8 %copy-done.5 = f32[256,2,8,8]{0,3,2,1:T(8,128)S(1)} copy-done((f32[256,2,8,8]{0,3,2,1:T(8,128)S(1)}, f32[256,2,8,8]{0,3,2,1:T(8,128)}, u32[]{:S(2)}) %copy-start.5) | copy-done | bytes 131096
  61.9 1.3 %fusion.68 = (f32[256,128]{0,1:T(8,128)S(1)}, f32[256,128]{0,1:T(8,128)S(1)}) fusion(f32[256,64]{0,1:T(8,128)S(1)} %get-tuple-element.106, f32[256,64]{0,1:T(8,128)S(1)} %get-tuple-element.105, f32[256,128]{0,1:T(8,128)S(1)} %convolution_add_fusion.3, f32[256,2,8,8]{0,3,2,1:T(8,128)S(1)} %copy-done.6, f32[256,2,8,8]{0,3,2,1:T(8,128)S(1)} %get-tuple-element.147, ...), kind=kLoop, calls=%fused_computation.148 | loop fusion | flops 983040 | bytes 1314304 | tf_op jit(solution)/shard_map/add | solution.py:156
  63.6 1.6 %collective-permute-start.4 = (f32[256,128]{0,1:T(8,128)S(1)}, f32[256,128]{0,1:T(8,128)S(1)}, u32[]{:S(2)}, u32[]{:S(2)}) collective-permute-start(f32[256,128]{0,1:T(8,128)S(1)} %copy.111), channel_id=1, source_target_pairs={{0,16},{16,0},{8,24},{24,8},{1,17},{17,1},{9,25},{25,9},{2,18},{18... | collective-permute-start | bytes 393224 | tf_op jit(solution)/shard_map/ppermute | solution.py:18
  66.2 2.4 %collective-permute-done.4 = f32[256,128]{0,1:T(8,128)S(1)} collective-permute-done((f32[256,128]{0,1:T(8,128)S(1)}, f32[256,128]{0,1:T(8,128)S(1)}, u32[]{:S(2)}, u32[]{:S(2)}) %collective-permute-start.4) | collective-permute-done | bytes 131104 | tf_op jit(solution)/shard_map/ppermute | solution.py:18
  70.3 0.8 %fusion.190 = f32[256,128]{0,1:T(8,128)S(1)} fusion(f32[128,128]{1,0:T(8,128)S(1)} %copy-done.1, f32[256,128]{0,1:T(8,128)S(1)} %get-tuple-element.53, f32[256,128]{0,1:T(8,128)S(1)} %get-tuple-element.82, f32[256,64]{0,1:T(8,128)S(1)} %get-tuple-element.104, f32[256,64]{0,1:T(8,128)S(1)} %get-tuple-element.103, f32[128]{0:T(128)S(1)} %copy-done.11), kind=kOutput, calls=%fused_computation.324 | convolution fusion | flops 50495488 | bytes 590336 | tf_op jit(solution)/shard_map/dot_general | solution.py:184
  71.9 1.3 %fusion.70 = (f32[256,128]{0,1:T(8,128)S(1)}, f32[256,128]{0,1:T(8,128)S(1)}) fusion(f32[256,64]{0,1:T(8,128)S(1)} %get-tuple-element.98, f32[256,64]{0,1:T(8,128)S(1)} %get-tuple-element.97, f32[256,128]{0,1:T(8,128)S(1)} %convolution_add_fusion.1, f32[256,2,8,8]{0,3,2,1:T(8,128)S(1)} %get-tuple-element.144, f32[256,2,8,8]{0,3,2,1:T(8,128)S(1)} %get-tuple-element.137, ...), kind=kLoop, calls=%fused_computation.154 | loop fusion | flops 983040 | bytes 1314304 | tf_op jit(solution)/shard_map/add | solution.py:156
  (220 shorter events, 25.9 us)
Async XLA Ops:
  1.8 13.9 %collective-permute-start = (f32[256,128]{0,1:T(8,128)}, f32[256,128]{0,1:T(8,128)}, u32[]{:S(2)}, u32[]{:S(2)}) collective-permute-start(f32[256,128]{0,1:T(8,128)} %copy.94), channel_id=1, source_target_pairs={{0,1},{1,0},{2,3},{3,2},{4,5},{5,4},{6,7},{7,6},{8,9},{9,8},{10,11... | collective-permute-start | bytes 393224 | tf_op jit(solution)/shard_map/ppermute | solution.py:18
  2.4 12.0 %copy-start.30 = (f32[256]{0:T(256)}, f32[256]{0:T(256)S(1)}, u32[]{:S(2)}) copy-start(f32[256]{0:T(256)S(1)} %get-tuple-element.21) | copy-start | bytes 3076
  2.4 12.0 %copy-start.32 = (f32[256]{0:T(256)}, f32[256]{0:T(256)S(1)}, u32[]{:S(2)}) copy-start(f32[256]{0:T(256)S(1)} %get-tuple-element.288) | copy-start | bytes 3076
  2.4 12.0 %copy-start.34 = (f32[256]{0:T(256)}, f32[256]{0:T(256)S(1)}, u32[]{:S(2)}) copy-start(f32[256]{0:T(256)S(1)} %get-tuple-element.290) | copy-start | bytes 3076
  2.5 12.6 %copy-start.42 = (f32[256]{0:T(256)}, f32[256]{0:T(256)S(1)}, u32[]{:S(2)}) copy-start(f32[256]{0:T(256)S(1)} %get-tuple-element.33) | copy-start | bytes 3076
  2.5 12.6 %copy-start.44 = (f32[256]{0:T(256)}, f32[256]{0:T(256)S(1)}, u32[]{:S(2)}) copy-start(f32[256]{0:T(256)S(1)} %get-tuple-element.299) | copy-start | bytes 3076
  3.3 11.5 %copy-start.46 = (f32[256]{0:T(256)}, f32[256]{0:T(256)S(1)}, u32[]{:S(2)}) copy-start(f32[256]{0:T(256)S(1)} %get-tuple-element.388) | copy-start | bytes 3076
  3.3 11.5 %copy-start.48 = (f32[256]{0:T(256)}, f32[256]{0:T(256)S(1)}, u32[]{:S(2)}) copy-start(f32[256]{0:T(256)S(1)} %get-tuple-element.392) | copy-start | bytes 3076
  3.3 11.5 %copy-start.50 = (f32[256]{0:T(256)}, f32[256]{0:T(256)S(1)}, u32[]{:S(2)}) copy-start(f32[256]{0:T(256)S(1)} %get-tuple-element.395) | copy-start | bytes 3076
  3.5 11.9 %copy-start.38 = (f32[256]{0:T(256)}, f32[256]{0:T(256)S(1)}, u32[]{:S(2)}) copy-start(f32[256]{0:T(256)S(1)} %get-tuple-element.35) | copy-start | bytes 3076
  3.5 11.9 %copy-start.40 = (f32[256]{0:T(256)}, f32[256]{0:T(256)S(1)}, u32[]{:S(2)}) copy-start(f32[256]{0:T(256)S(1)} %get-tuple-element.303) | copy-start | bytes 3076
  3.6 11.5 %copy-start.28 = (f32[256]{0:T(256)}, f32[256]{0:T(256)S(1)}, u32[]{:S(2)}) copy-start(f32[256]{0:T(256)S(1)} %get-tuple-element.383) | copy-start | bytes 3076
  4.2 11.2 %copy-start.26 = (f32[256]{0:T(256)}, f32[256]{0:T(256)S(1)}, u32[]{:S(2)}) copy-start(f32[256]{0:T(256)S(1)} %get-tuple-element.380) | copy-start | bytes 3076
  23.2 2.8 %copy-start.13 = (f32[256,8]{0,1:T(8,128)S(1)}, f32[256,8]{0,1:T(8,128)}, u32[]{:S(2)}) copy-start(f32[256,8]{0,1:T(8,128)} %get-tuple-element.277) | copy-start | bytes 24580
  23.2 2.8 %copy-start.14 = (f32[256,8]{0,1:T(8,128)S(1)}, f32[256,8]{0,1:T(8,128)}, u32[]{:S(2)}) copy-start(f32[256,8]{0,1:T(8,128)} %get-tuple-element.278) | copy-start | bytes 24580
  23.2 2.8 %copy-start.15 = (f32[256,8]{0,1:T(8,128)S(1)}, f32[256,8]{0,1:T(8,128)}, u32[]{:S(2)}) copy-start(f32[256,8]{0,1:T(8,128)} %get-tuple-element.364) | copy-start | bytes 24580
  23.3 2.7 %copy-start.12 = (f32[256,8]{0,1:T(8,128)S(1)}, f32[256,8]{0,1:T(8,128)}, u32[]{:S(2)}) copy-start(f32[256,8]{0,1:T(8,128)} %get-tuple-element.276) | copy-start | bytes 24580
  23.3 6.8 %collective-permute-start.1 = (f32[256,128]{0,1:T(8,128)S(1)}, f32[256,128]{0,1:T(8,128)S(1)}, u32[]{:S(2)}, u32[]{:S(2)}) collective-permute-start(f32[256,128]{0,1:T(8,128)S(1)} %copy.117), channel_id=1, source_target_pairs={{0,2},{2,0},{1,3},{3,1},{4,6},{6,4},{5,7},{7,5},{8,10},{10,8},{9,1... | collective-permute-start | bytes 393224 | tf_op jit(solution)/shard_map/ppermute | solution.py:18
  34.2 1.0 %copy-start.9 = (f32[256,2,8,8]{0,3,2,1:T(8,128)S(1)}, f32[256,2,8,8]{0,3,2,1:T(8,128)}, u32[]{:S(2)}) copy-start(f32[256,2,8,8]{0,3,2,1:T(8,128)} %get-tuple-element.171) | copy-start | bytes 393220
  37.5 2.9 %copy-start.18 = (f32[256,8]{0,1:T(8,128)S(1)}, f32[256,8]{0,1:T(8,128)}, u32[]{:S(2)}) copy-start(f32[256,8]{0,1:T(8,128)} %get-tuple-element.371) | copy-start | bytes 24580
  37.5 2.9 %copy-start.21 = (f32[256,8]{0,1:T(8,128)S(1)}, f32[256,8]{0,1:T(8,128)}, u32[]{:S(2)}) copy-start(f32[256,8]{0,1:T(8,128)} %get-tuple-element.318) | copy-start | bytes 24580
  37.5 2.9 %copy-start.22 = (f32[256,8]{0,1:T(8,128)S(1)}, f32[256,8]{0,1:T(8,128)}, u32[]{:S(2)}) copy-start(f32[256,8]{0,1:T(8,128)} %get-tuple-element.358) | copy-start | bytes 24580
  37.5 2.9 %copy-start.23 = (f32[256,8]{0,1:T(8,128)S(1)}, f32[256,8]{0,1:T(8,128)}, u32[]{:S(2)}) copy-start(f32[256,8]{0,1:T(8,128)} %get-tuple-element.366) | copy-start | bytes 24580
  37.5 9.1 %collective-permute-start.2 = (f32[256,128]{0,1:T(8,128)S(1)}, f32[256,128]{0,1:T(8,128)S(1)}, u32[]{:S(2)}, u32[]{:S(2)}) collective-permute-start(f32[256,128]{0,1:T(8,128)S(1)} %select_bitcast_fusion), channel_id=1, source_target_pairs={{0,4},{4,0},{1,5},{5,1},{2,6},{6,2},{3,7},{7,3},{8,12},{12,8},{9,1... | collective-permute-start | bytes 393224 | tf_op jit(solution)/shard_map/ppermute | solution.py:18
  52.5 1.7 %copy-start.16 = (f32[256,8]{0,1:T(8,128)S(1)}, f32[256,8]{0,1:T(8,128)}, u32[]{:S(2)}) copy-start(f32[256,8]{0,1:T(8,128)} %get-tuple-element.370) | copy-start | bytes 24580
  52.6 1.7 %copy-start.17 = (f32[256,8]{0,1:T(8,128)S(1)}, f32[256,8]{0,1:T(8,128)}, u32[]{:S(2)}) copy-start(f32[256,8]{0,1:T(8,128)} %get-tuple-element.317) | copy-start | bytes 24580
  52.6 1.6 %copy-start.19 = (f32[256,8]{0,1:T(8,128)S(1)}, f32[256,8]{0,1:T(8,128)}, u32[]{:S(2)}) copy-start(f32[256,8]{0,1:T(8,128)} %get-tuple-element.359) | copy-start | bytes 24580
  52.6 1.6 %copy-start.20 = (f32[256,8]{0,1:T(8,128)S(1)}, f32[256,8]{0,1:T(8,128)}, u32[]{:S(2)}) copy-start(f32[256,8]{0,1:T(8,128)} %get-tuple-element.365) | copy-start | bytes 24580
  52.7 5.0 %collective-permute-start.3 = (f32[256,128]{0,1:T(8,128)S(1)}, f32[256,128]{0,1:T(8,128)S(1)}, u32[]{:S(2)}, u32[]{:S(2)}) collective-permute-start(f32[256,128]{0,1:T(8,128)S(1)} %copy.105), channel_id=1, source_target_pairs={{0,8},{8,0},{16,24},{24,16},{1,9},{9,1},{17,25},{25,17},{2,10},{10... | collective-permute-start | bytes 393224 | tf_op jit(solution)/shard_map/ppermute | solution.py:18
  63.5 1.7 %copy-start.36 = (f32[256]{0:T(256)S(1)}, f32[256]{0:T(256)}, u32[]{:S(2)}) copy-start(f32[256]{0:T(256)} %get-tuple-element.37) | copy-start | bytes 3076
  63.5 1.7 %copy-start.37 = (f32[256]{0:T(256)S(1)}, f32[256]{0:T(256)}, u32[]{:S(2)}) copy-start(f32[256]{0:T(256)} %get-tuple-element.308) | copy-start | bytes 3076
  63.6 5.0 %collective-permute-start.4 = (f32[256,128]{0,1:T(8,128)S(1)}, f32[256,128]{0,1:T(8,128)S(1)}, u32[]{:S(2)}, u32[]{:S(2)}) collective-permute-start(f32[256,128]{0,1:T(8,128)S(1)} %copy.111), channel_id=1, source_target_pairs={{0,16},{16,0},{8,24},{24,8},{1,17},{17,1},{9,25},{25,9},{2,18},{18... | collective-permute-start | bytes 393224 | tf_op jit(solution)/shard_map/ppermute | solution.py:18
  (30 other events, 24.7 us)
where the time goes:
time: 74.8 us; the launch traced here: 74.2 us
  other arithmetic  20 us (27%)
  waiting for transfers between devices  16 us (21%)
  matrix products  15.4 us (21%)
  local copies, waits for them, and re-layouts  12.5 us (17%)
  starting transfers between devices  8.98 us (12%)
  between operations  1.34 us (2%)
    ppermute x5, waiting for transfers between devices, from_partner(): return lax.ppermute(block, axis, route)  16 us
    dot_general x20, matrix products, combine(): jnp.dot(stacked, merge_table, precision=lax.Precision.HIGHEST, preferred_...  15.4 us
    ppermute x5, starting transfers between devices, from_partner(): return lax.ppermute(block, axis, route)  8.98 us
    unnamed x114, local copies, waits for them, and re-layouts  8.56 us
    add x4, other arithmetic, rotate(): return values * cosine + swapped * (sine_part * sign_pattern)  5.49 us
    add x5, other arithmetic, phase_cycles(): coeff_one = (2.0 + sine_one * sine_two) / 16.0  2.11 us
    add x5, other arithmetic, phase_cycles(): coeff_two = (2.0 + cosine_one * cosine_two) / 16.0  2.07 us
    another operation x6, other arithmetic, join_pairs(): jnp.stack([branch_out.reshape(high_count, low_span, 128) for branch_out i...  1.88 us
  transfers between devices with their start and end apart: 5, of which 4 were waited for; matrix products, arithmetic and copies ran while one was open for 15% of the time, Pallas kernels for 0%

commit v1 on v0

v1 whole, which is shorter than its diff:
```python
import functools

import jax
import jax.numpy as jnp
import numpy as np
from jax import lax
from jax.experimental import pallas as pl
from jax.experimental.pallas import tpu as pltpu
from jax.sharding import PartitionSpec as P

GRID_N = 16384
TREE_LEVELS = 11
LOW_BITS = 4
BLOCK = 1 << LOW_BITS


def chebyshev_nodes():
    return 0.5 * np.cos(np.pi * (2.0 * np.arange(8) + 1.0) / 16.0)


def lagrange_weights(which_child):
    node_values = chebyshev_nodes()
    targets = (node_values + which_child - 0.5) / 2.0
    weights_table = np.ones((8, 8))
    for anchor in range(8):
        for other_node in range(8):
            if other_node != anchor:
                weights_table[anchor, :] = (
                    weights_table[anchor, :]
                    * (targets - node_values[other_node])
                    / (node_values[anchor] - node_values[other_node])
                )
    return weights_table


def merge_matrix(dimension):
    merge_table = np.zeros((256, 128))
    for which_child in range(2):
        weights_table = lagrange_weights(which_child)
        if dimension == 0:
            block_table = np.kron(weights_table, np.eye(8))
        else:
            block_table = np.kron(np.eye(8), weights_table)
        for half in range(2):
            first = half * 128 + which_child * 64
            merge_table[first : first + 64, half * 64 : half * 64 + 64] = block_table.T
    return merge_table


def split_matrices():
    parts = []
    for dimension in range(2):
        exact = merge_matrix(dimension).astype(np.float32)
        high = exact.astype(jnp.bfloat16)
        low = (exact - high.astype(np.float32)).astype(jnp.bfloat16)
        parts += [high, low]
    return np.stack(parts)


def lane_nodes():
    lanes = np.arange(128) % 64
    nodes = chebyshev_nodes()
    return np.stack([nodes[lanes // 8], nodes[lanes % 8]] + [np.zeros(128)] * 6).astype(np.float32)


def level_plan(local_bits, inner_bits, outer_bits):
    levels_total = inner_bits + outer_bits
    carried = [local_bits + level for level in range(levels_total)]
    moved = [
        local_bits - inner_bits + level
        if level < inner_bits
        else local_bits - levels_total + level - inner_bits
        for level in range(levels_total)
    ]
    source = [[], []]
    for level in range(levels_total):
        source[(level + 1) % 2].append(("carried", level))
    source[0] += [local_bits - 7, local_bits - 6, local_bits - 5]
    source[1] += [local_bits - 4, local_bits - 3, local_bits - 2, local_bits - 1]
    target = [[], []]
    for ordinal in range(local_bits - 7):
        target[ordinal % 2].append(ordinal)

    def place(bit):
        if isinstance(bit, tuple):
            return moved[bit[1]]
        if bit in moved:
            return (moved.index(bit),)
        return bit

    source = [[place(bit) for bit in group] for group in source]
    target = [[place(bit) for bit in group] for group in target]
    plan = []
    for level in range(levels_total):
        dimension = (level + 1) % 2
        plan.append(
            (dimension, moved[level], [list(g) for g in target], [list(g) for g in source])
        )
        source[dimension] = source[dimension][1:]
        target[dimension] = [moved[level]] + target[dimension]
    plan.append((None, None, [list(g) for g in target], [list(g) for g in source]))
    return plan


def box_span(source):
    return GRID_N * 2.0 ** (len(source) - TREE_LEVELS)


def sincos(turns):
    near = turns - jnp.floor(turns + 0.5)
    square = near * near
    root = np.sqrt(2.0)
    sine = SINE[3] * root
    for coefficient in SINE[2::-1]:
        sine = sine * square + coefficient * root
    sine = sine * near
    cosine = COSINE[4] * root
    for coefficient in COSINE[3::-1]:
        cosine = cosine * square + coefficient * root
    return sine * cosine, 1.0 - sine * sine


def fit(function, powers):
    grid = 0.25 * (1.0 - np.cos(np.pi * (np.arange(4000) + 0.5) / 4000))
    matrix = np.stack([grid**power for power in powers], 1)
    return [float(v) for v in np.linalg.lstsq(matrix, function(np.pi * grid), rcond=None)[0]]


SINE = fit(np.sin, (1, 3, 5, 7))
COSINE = fit(np.cos, (0, 2, 4, 6, 8))


def combos(bits):
    result = [{}]
    for bit in bits:
        result = [{**one, bit: value} for one in result for value in range(2)]
    return result


def pick(assignment, bits):
    return tuple(assignment[bit] for bit in bits)


def kernel(plan, row_bits, axes, x_ref, matrix_ref, node_ref, out_ref, high_ref, low_ref):
    inner_size = lax.axis_size(axes[1])
    device = lax.axis_index(axes[0]) * inner_size + lax.axis_index(axes[1])
    leading = list(range(row_bits - 1, LOW_BITS - 1, -1))
    rows = lax.broadcasted_iota(jnp.int32, (BLOCK, 128), 0)
    lanes = lax.broadcasted_iota(jnp.int32, (BLOCK, 128), 1)
    low_half = lanes < 64
    child = jnp.where(low_half, 0.0, 1.0)
    row_bit = [(rows >> bit & 1).astype(jnp.float32) for bit in range(LOW_BITS)]
    node = [jnp.broadcast_to(node_ref[d : d + 1, :], (BLOCK, 128)) for d in range(2)]
    device_bit = {}

    def index_tile(places, start):
        total = start
        scalar = None
        for ordinal, where in enumerate(places):
            weight = float(1 << ordinal)
            if isinstance(where, tuple):
                if where[0] not in device_bit:
                    device_bit[where[0]] = (device >> where[0] & 1).astype(jnp.float32)
                term = device_bit[where[0]] * weight
                scalar = term if scalar is None else scalar + term
            elif where < LOW_BITS:
                total = total + row_bit[where] * weight
        return total if scalar is None else total + scalar

    def index_lead(places, assignment):
        return sum(
            float(1 << ordinal) * assignment[where]
            for ordinal, where in enumerate(places)
            if not isinstance(where, tuple) and where in assignment
        )

    def lead_bits(places, free):
        return [w for w in places if not isinstance(w, tuple) and w in free]

    def coefficients(source, free, lane_child):
        trig = []
        bits = [lead_bits(source[d], free) for d in range(2)]
        for d in range(2):
            width = 2.0 ** (-len(source[d]))
            start = node[d] + 0.5
            if lane_child == d:
                start = start + child
            tile = index_tile(source[d], start) * width
            trig.append(
                {
                    pick(one, bits[d]): sincos(tile + index_lead(source[d], one) * width)
                    for one in combos(bits[d])
                }
            )
        table = {}
        for one in combos(bits[0]):
            for two in combos(bits[1]):
                sine_one, cosine_one = trig[0][pick(one, bits[0])]
                sine_two, cosine_two = trig[1][pick(two, bits[1])]
                first = 0.125 + sine_one * sine_two * 0.0625
                second = 0.125 + cosine_one * cosine_two * 0.0625
                table[pick(one, bits[0]), pick(two, bits[1])] = (first * first, second * second)
        return table, bits

    def frequencies(target, source, free):
        result = []
        for d in range(2):
            bits = lead_bits(target[d], free)
            width = box_span(source[d])
            tile = index_tile(target[d], 0.5 * jnp.ones((BLOCK, 128), jnp.float32)) * width
            result.append(
                (
                    bits,
                    {
                        pick(one, bits): tile + (index_lead(target[d], one) * width - GRID_N / 2.0)
                        for one in combos(bits)
                    },
                )
            )
        return result

    def root(value):
        return value * lax.rsqrt(value)

    def pack(first, second):
        return (
            jnp.where(low_half, first, pltpu.roll(second, 64, 1)),
            jnp.where(low_half, pltpu.roll(first, 64, 1), second),
        )

    first_moved = plan[0][1]
    state = {}
    for one in combos([bit for bit in leading if bit != first_moved]):
        halves = []
        for value in range(2):
            full = {**one, first_moved: value}
            start = sum(full[bit] << bit for bit in leading)
            halves.append(x_ref[start : start + BLOCK, :])
        state[pick(one, [b for b in leading if b != first_moved])] = pack(*halves)

    for level, (dimension, moved, target, source) in enumerate(plan[:-1]):
        last = level == len(plan) - 2
        free = [bit for bit in leading if bit != moved]
        if last:
            next_moved = free[0]
        else:
            next_moved = plan[level + 1][1]
        next_free = [bit for bit in leading if bit != next_moved]
        table, source_lead = coefficients(source, free, dimension)
        parents = frequencies(target, source, free)
        quarter = 0.25 * box_span(source[dimension])
        children = [
            {key: value + shift for key, value in parents[dimension][1].items()}
            for shift in (-quarter, quarter)
        ]
        other = 1 - dimension
        slots = {}
        for position, one in enumerate(combos(next_free)):
            slots[pick(one, next_free)] = position
        half_rows = len(slots) * BLOCK
        for one in combos(free):
            real, imaginary = state[pick(one, free)]
            squares = table[pick(one, source_lead[0]), pick(one, source_lead[1])]
            key = [pick(one, parents[d][0]) for d in range(2)]
            k_other = parents[other][1][key[other]]
            k_parent = parents[dimension][1][key[dimension]]
            fixed = squares[other] * (k_other * k_other)
            if level > 0:
                radius = root(fixed + squares[dimension] * (k_parent * k_parent))
            for branch in range(2):
                k_child = children[branch][key[dimension]]
                turns = root(fixed + squares[dimension] * (k_child * k_child))
                if level > 0:
                    scale = 2.0 ** (-len(source[dimension])) * (-quarter, quarter)[branch]
                    turns = (turns - radius) + node[dimension] * scale
                else:
                    turns = turns - jnp.floor(turns)
                    width = [2.0 ** (-len(source[d])) for d in range(2)]
                    turns = turns + (
                        node[dimension] * width[dimension] * k_child
                        + node[other] * width[other] * k_other
                    )
                sine, cosine = sincos(turns)
                full = {**one, moved: branch}
                column = full[next_moved] * 128
                slot = slots[pick(full, next_free)] * BLOCK
                for component, value in enumerate(
                    (real * cosine - imaginary * sine, real * sine + imaginary * cosine)
                ):
                    top = value.astype(jnp.bfloat16)
                    rest = (value - top.astype(jnp.float32)).astype(jnp.bfloat16)
                    place = pl.ds(component * half_rows + slot, BLOCK)
                    high_ref[place, column : column + 128] = top
                    low_ref[place, column : column + 128] = rest
        top, rest = matrix_ref[2 * dimension], matrix_ref[2 * dimension + 1]

        def product(a, b):
            return jnp.dot(a, b, preferred_element_type=jnp.float32)

        merged = product(high_ref[...], top) + product(low_ref[...], top) + product(high_ref[...], rest)
        state = {
            key: (
                merged[slot * BLOCK : (slot + 1) * BLOCK],
                merged[half_rows + slot * BLOCK : half_rows + (slot + 1) * BLOCK],
            )
            for key, slot in slots.items()
        }

    _, _, target, source = plan[-1]
    packed = next_moved
    free = [bit for bit in leading if bit != packed]
    lane_part = [[], []]
    for d in range(2):
        for name, places in (("a", target[d]), ("b", source[d])):
            for ordinal, where in enumerate(places):
                if where == packed:
                    lane_part[d].append((name, float(1 << ordinal)))
    trig, bits = [], [lead_bits(source[d], free) for d in range(2)]
    for d in range(2):
        width = 2.0 ** (-len(source[d]))
        start = node[d] + 0.5
        for name, weight in lane_part[d]:
            if name == "b":
                start = start + child * weight
        tile = index_tile(source[d], start) * width
        trig.append(
            {pick(one, bits[d]): sincos(tile + index_lead(source[d], one) * width) for one in combos(bits[d])}
        )
    centers = frequencies(target, source, free)
    for d in range(2):
        for name, weight in lane_part[d]:
            if name == "a":
                step = child * (weight * box_span(source[d]))
                centers[d] = (centers[d][0], {k: v + step for k, v in centers[d][1].items()})
    for one in combos(free):
        sine_one, cosine_one = trig[0][pick(one, bits[0])]
        sine_two, cosine_two = trig[1][pick(one, bits[1])]
        first = 0.125 + sine_one * sine_two * 0.0625
        second = 0.125 + cosine_one * cosine_two * 0.0625
        k = [centers[d][1][pick(one, centers[d][0])] for d in range(2)]
        first, second = first * k[0], second * k[1]
        turns = root(first * first + second * second)
        turns = turns - jnp.floor(turns)
        width = [2.0 ** (-len(source[d])) for d in range(2)]
        turns = turns + (node[0] * width[0] * k[0] + node[1] * width[1] * k[1])
        sine, cosine = sincos(turns)
        real, imaginary = state[pick(one, free)]
        outputs = pack(real * cosine + imaginary * sine, imaginary * cosine - real * sine)
        for value in range(2):
            full = {**one, packed: value}
            start = sum(full[bit] << bit for bit in leading)
            out_ref[start : start + BLOCK, :] = outputs[value]


def run_levels(rows, plan):
    row_bits = rows.shape[0].bit_length() - 1
    half = rows.shape[0]
    vmem = pl.BlockSpec(memory_space=pltpu.VMEM)
    return pl.pallas_call(
        functools.partial(kernel, plan, row_bits, ("outer", "inner")),
        out_shape=jax.ShapeDtypeStruct(rows.shape, jnp.float32),
        in_specs=[vmem] * 3,
        out_specs=vmem,
        scratch_shapes=[pltpu.VMEM((half, 256), jnp.bfloat16)] * 2,
        compiler_params=pltpu.CompilerParams(vmem_limit_bytes=32 * 1024 * 1024),
    )(rows, jnp.asarray(split_matrices()), jnp.asarray(lane_nodes()))


def reorder_plan(plan, order):
    def place(bit):
        return bit if bit is None or isinstance(bit, tuple) else order.index(bit)

    return [
        (dimension, place(moved), [[place(b) for b in g] for g in target], [[place(b) for b in g] for g in source])
        for dimension, moved, target, source in plan
    ]


def reorder_rows(rows, order):
    count = len(order)
    if list(order) == list(range(count)):
        return rows
    axes = [count - 1 - order[count - 1 - i] for i in range(count)]
    return rows.reshape((2,) * count + (128,)).transpose(axes + [count]).reshape(rows.shape)


def body(weights):
    row_bits = weights.shape[0].bit_length() - 1
    inner_bits = lax.axis_size("inner").bit_length() - 1
    outer_bits = lax.axis_size("outer").bit_length() - 1
    plan = level_plan(row_bits, inner_bits, outer_bits)
    moved = [entry[1] for entry in plan[:-1]]
    rows = lax.all_to_all(weights, ("inner", "outer"), 0, 0, tiled=True)
    level = 0
    while level < len(moved):
        count = 1
        while level + count < len(moved) and count < row_bits - LOW_BITS:
            count += 1
        group = moved[level : level + count]
        order = [bit for bit in range(row_bits) if bit not in group] + sorted(group)
        rows = reorder_rows(rows, order)
        rows = run_levels(rows, reorder_plan(plan[level : level + count + 1], order))
        back = [order.index(bit) for bit in range(row_bits)]
        rows = reorder_rows(rows, back)
        level += count
    return rows


def solution(mesh):
    spec = P(("outer", "inner"), None)
    return jax.shard_map(body, mesh=mesh, in_specs=(spec,), out_specs=spec, check_vma=False)
```

time: 74.8 us -> 22.8 us (0.30)
  other arithmetic: 20 us -> 0 us
  blocking collectives: 0 us -> 18.3 us
  waiting for transfers between devices: 16 us -> 0 us
  matrix products: 15.4 us -> 0 us
  local copies, waits for them, and re-layouts: 12.5 us -> 0.01 us
  starting transfers between devices: 8.98 us -> 0 us
  Pallas kernels: 0 us -> 4.33 us
  between operations: 1.34 us -> 0.01 us
    all_to_all x0 -> x1, blocking collectives: none -> 18.3 us  [body(): rows = lax.all_to_all(weights, ('inner', 'outer'), 0, 0, tiled=True)]
    ppermute x5 -> x0, waiting for transfers between devices: 16 us -> none  [from_partner(): return lax.ppermute(block, axis, route)]
    dot_general x20 -> x0, matrix products: 15.4 us -> none  [combine(): jnp.dot(stacked, merge_table, precision=lax.Precision.HIGHEST, preferred_...]
    add x24 -> x0, other arithmetic: 10.6 us -> none  [the longest x4 5.49 us: rotate(): return values * cosine + swapped * (sine_part * sign_pattern)]
    ppermute x5 -> x0, starting transfers between devices: 8.98 us -> none  [from_partner(): return lax.ppermute(block, axis, route)]
    unnamed x114 -> x4, local copies, waits for them, and re-layouts: 8.56 us -> 0.01 us
    pallas_call x0 -> x1, Pallas kernels: none -> 4.33 us  [run_levels(): pl.pallas_call(functools.partial(kernel, plan, row_bits, ('outer', 'inner...]
    mul x15 -> x0, other arithmetic: 3.54 us -> none  [the longest x5 1.41 us: rotate(): radians = 2.0 * np.pi * cycles]
  transfers between devices with their start and end apart: 5 -> 0, of which waited for: 4 -> 0; matrix products, arithmetic and copies ran while one was open for 15% -> 0% of each run, Pallas kernels for 0% -> 0%
where the time goes in v1:
time: 22.8 us; the launch traced here: 22.6 us
  blocking collectives  18.3 us (80%)
  Pallas kernels  4.33 us (19%)
    all_to_all x1, blocking collectives, body(): rows = lax.all_to_all(weights, ('inner', 'outer'), 0, 0, tiled=True)  18.3 us
    pallas_call x1, Pallas kernels, run_levels(): pl.pallas_call(functools.partial(kernel, plan, row_bits, ('outer', 'inner...  4.33 us

profile of v1, /device:TPU:0, one launch (start us, length us, event | category | flops | bytes accessed | tf_op | source)
XLA Modules:
  0.0 22.6 jit_solution(11645673421586964569)
XLA Ops:
  0.0 0.0 copy-start
  0.0 0.0 copy-start.1
  0.0 18.3 %all_to_all.11 = f32[32,16,128]{2,1,0:T(8,128)S(1)} all-to-all(f32[32,16,128]{2,1,0:T(8,128)} %bitcast.3), channel_id=1, replica_groups=mesh['outer'=4,'inner'=8] {'inner','outer'}, dimensions={0} | all-to-all | bytes 524288 | tf_op jit(solution)/shard_map/all_to_all | solution.py:393
  18.3 0.0 copy-done
  18.3 0.0 copy-done.1
  18.3 4.3 %shard_map.37 = f32[512,128]{1,0:T(8,128)} custom-call(f32[512,128]{1,0:T(8,128)S(1)} %bitcast.2, bf16[4,256,128]{2,1,0:T(8,128)(2,1)S(1)} %copy-done, f32[8,128]{1,0:T(8,128)S(1)} %copy-done.1), custom_call_target="tpu_custom_call" | custom-call | tf_op jit(solution)/shard_map/pallas_call | solution.py:359
Async XLA Ops:
  0.0 18.3 %copy-start = (bf16[4,256,128]{2,1,0:T(8,128)(2,1)S(1)}, bf16[4,256,128]{2,1,0:T(8,128)(2,1)}, u32[]{:S(2)}) copy-start(bf16[4,256,128]{2,1,0:T(8,128)(2,1)} %constant.4.clone.matrix_ref) | copy-start | bytes 786436
  0.0 18.3 %copy-start.1 = (f32[8,128]{1,0:T(8,128)S(1)}, f32[8,128]{1,0:T(8,128)}, u32[]{:S(2)}) copy-start(f32[8,128]{1,0:T(8,128)} %constant.5.clone.node_ref) | copy-start | bytes 12292

commit v2 on v1

--- a/solution.py
+++ b/solution.py
@@ -53,7 +53,7 @@
         exact = merge_matrix(dimension).astype(np.float32)
         high = exact.astype(jnp.bfloat16)
         low = (exact - high.astype(np.float32)).astype(jnp.bfloat16)
-        parts += [high, low]
+        parts.append(np.concatenate([high, low], 1))
     return np.stack(parts)
 
 
@@ -106,28 +106,54 @@
     return GRID_N * 2.0 ** (len(source) - TREE_LEVELS)
 
 
+def reduced(turns):
+    return turns - jnp.floor(turns + 0.5)
+
+
+def odd_series(coefficients, near, square):
+    total = coefficients[-1]
+    for coefficient in coefficients[-2::-1]:
+        total = total * square + coefficient
+    return total * near
+
+
 def sincos(turns):
-    near = turns - jnp.floor(turns + 0.5)
+    near = reduced(turns)
     square = near * near
-    root = np.sqrt(2.0)
-    sine = SINE[3] * root
-    for coefficient in SINE[2::-1]:
-        sine = sine * square + coefficient * root
-    sine = sine * near
-    cosine = COSINE[4] * root
-    for coefficient in COSINE[3::-1]:
-        cosine = cosine * square + coefficient * root
+    sine = odd_series(SINE, near, square)
+    cosine = odd_series(COSINE, 1.0, square)
     return sine * cosine, 1.0 - sine * sine
 
 
+def rotation(turns):
+    near = reduced(turns)
+    sine = odd_series(SHORT_SINE, near, near * near)
+    square = sine * sine
+    rest = 2.0 - square
+    return sine * (rest * lax.rsqrt(rest)), 1.0 - square
+
+
 def fit(function, powers):
-    grid = 0.25 * (1.0 - np.cos(np.pi * (np.arange(4000) + 0.5) / 4000))
+    grid = 0.25 * (1.0 - np.cos(np.pi * (np.arange(2000) + 0.5) / 2000))
     matrix = np.stack([grid**power for power in powers], 1)
-    return [float(v) for v in np.linalg.lstsq(matrix, function(np.pi * grid), rcond=None)[0]]
-
-
-SINE = fit(np.sin, (1, 3, 5, 7))
-COSINE = fit(np.cos, (0, 2, 4, 6, 8))
+    exact = np.sqrt(2.0) * function(np.pi * grid)
+    weight = np.ones_like(grid)
+    best = None
+    for _ in range(100):
+        scale = np.sqrt(weight)
+        solved = np.linalg.lstsq(matrix * scale[:, None], exact * scale, rcond=None)[0]
+        error = np.abs(matrix @ solved - exact)
+        if best is None or error.max() < best[0]:
+            best = (error.max(), solved)
+        weight = weight * error
+        weight = weight / weight.sum()
+    return best[1], best[0]
+
+
+SINE = [float(v) for v in fit(np.sin, (1, 3, 5, 7, 9))[0]]
+COSINE = [float(v) for v in fit(np.cos, (0, 2, 4, 6, 8))[0]]
+SHORT_SINE, SHORT_ERROR = fit(np.sin, (1, 3, 5, 7))
+SHORT_SINE = [float(v) for v in SHORT_SINE * (1.0 - SHORT_ERROR - 6e-7)]
 
 
 def combos(bits):
@@ -141,7 +167,7 @@
     return tuple(assignment[bit] for bit in bits)
 
 
-def kernel(plan, row_bits, axes, x_ref, matrix_ref, node_ref, out_ref, high_ref, low_ref):
+def kernel(plan, row_bits, axes, x_ref, matrix_ref, node_ref, out_ref):
     inner_size = lax.axis_size(axes[1])
     device = lax.axis_index(axes[0]) * inner_size + lax.axis_index(axes[1])
     leading = list(range(row_bits - 1, LOW_BITS - 1, -1))
@@ -254,11 +280,8 @@
             for shift in (-quarter, quarter)
         ]
         other = 1 - dimension
-        slots = {}
-        for position, one in enumerate(combos(next_free)):
-            slots[pick(one, next_free)] = position
-        half_rows = len(slots) * BLOCK
-        for one in combos(free):
+        def rotated(one):
+            results = []
             real, imaginary = state[pick(one, free)]
             squares = table[pick(one, source_lead[0]), pick(one, source_lead[1])]
             key = [pick(one, parents[d][0]) for d in range(2)]
@@ -267,12 +290,13 @@
             fixed = squares[other] * (k_other * k_other)
             if level > 0:
                 radius = root(fixed + squares[dimension] * (k_parent * k_parent))
+                step = node[dimension] * (2.0 ** (-len(source[dimension])) * quarter)
+                offsets = (radius + step, radius - step)
             for branch in range(2):
                 k_child = children[branch][key[dimension]]
                 turns = root(fixed + squares[dimension] * (k_child * k_child))
                 if level > 0:
-                    scale = 2.0 ** (-len(source[dimension])) * (-quarter, quarter)[branch]
-                    turns = (turns - radius) + node[dimension] * scale
+                    turns = turns - offsets[branch]
                 else:
                     turns = turns - jnp.floor(turns)
                     width = [2.0 ** (-len(source[d])) for d in range(2)]
@@ -280,31 +304,46 @@
                         node[dimension] * width[dimension] * k_child
                         + node[other] * width[other] * k_other
                     )
-                sine, cosine = sincos(turns)
-                full = {**one, moved: branch}
-                column = full[next_moved] * 128
-                slot = slots[pick(full, next_free)] * BLOCK
-                for component, value in enumerate(
-                    (real * cosine - imaginary * sine, real * sine + imaginary * cosine)
-                ):
-                    top = value.astype(jnp.bfloat16)
-                    rest = (value - top.astype(jnp.float32)).astype(jnp.bfloat16)
-                    place = pl.ds(component * half_rows + slot, BLOCK)
-                    high_ref[place, column : column + 128] = top
-                    low_ref[place, column : column + 128] = rest
-        top, rest = matrix_ref[2 * dimension], matrix_ref[2 * dimension + 1]
-
-        def product(a, b):
-            return jnp.dot(a, b, preferred_element_type=jnp.float32)
-
-        merged = product(high_ref[...], top) + product(low_ref[...], top) + product(high_ref[...], rest)
-        state = {
-            key: (
-                merged[slot * BLOCK : (slot + 1) * BLOCK],
-                merged[half_rows + slot * BLOCK : half_rows + (slot + 1) * BLOCK],
-            )
-            for key, slot in slots.items()
-        }
+                sine, cosine = rotation(turns)
+                results.append((real * cosine - imaginary * sine, real * sine + imaginary * cosine))
+            return results
+
+        later = {bit: place for place, (_, bit, _, _) in enumerate(plan[:-1])}
+        order = sorted(
+            (bit for bit in next_free if bit != moved),
+            key=lambda bit: -later.get(bit, len(plan)) if later.get(bit, len(plan)) > level else 0,
+        )
+        matrix = matrix_ref[dimension]
+        next_state = {}
+        for group in combos(order):
+            terms = {}
+            for half in range(2):
+                one = {**group, next_moved: half}
+                for branch, values in enumerate(rotated(one)):
+                    for component, value in enumerate(values):
+                        top = value.astype(jnp.bfloat16)
+                        rest = (value - top.astype(jnp.float32)).astype(jnp.bfloat16)
+                        terms[branch, component, half] = (top, rest)
+            total = None
+            for part in range(2):
+                stacked = jnp.concatenate(
+                    [
+                        jnp.concatenate([terms[branch, component, half][part] for half in range(2)], 1)
+                        for branch in range(2)
+                        for component in range(2)
+                    ],
+                    0,
+                )
+                product = jnp.dot(stacked, matrix, preferred_element_type=jnp.float32)
+                total = product if total is None else total + product
+            total = total[:, :128] + total[:, 128:]
+            for branch in range(2):
+                first = 2 * branch * BLOCK
+                next_state[pick({**group, moved: branch}, next_free)] = (
+                    total[first : first + BLOCK],
+                    total[first + BLOCK : first + 2 * BLOCK],
+                )
+        state = next_state
 
     _, _, target, source = plan[-1]
     packed = next_moved
@@ -343,7 +382,7 @@
         turns = turns - jnp.floor(turns)
         width = [2.0 ** (-len(source[d])) for d in range(2)]
         turns = turns + (node[0] * width[0] * k[0] + node[1] * width[1] * k[1])
-        sine, cosine = sincos(turns)
+        sine, cosine = rotation(turns)
         real, imaginary = state[pick(one, free)]
         outputs = pack(real * cosine + imaginary * sine, imaginary * cosine - real * sine)
         for value in range(2):
@@ -354,14 +393,12 @@
 
 def run_levels(rows, plan):
     row_bits = rows.shape[0].bit_length() - 1
-    half = rows.shape[0]
     vmem = pl.BlockSpec(memory_space=pltpu.VMEM)
     return pl.pallas_call(
         functools.partial(kernel, plan, row_bits, ("outer", "inner")),
         out_shape=jax.ShapeDtypeStruct(rows.shape, jnp.float32),
         in_specs=[vmem] * 3,
         out_specs=vmem,
-        scratch_shapes=[pltpu.VMEM((half, 256), jnp.bfloat16)] * 2,
         compiler_params=pltpu.CompilerParams(vmem_limit_bytes=32 * 1024 * 1024),
     )(rows, jnp.asarray(split_matrices()), jnp.asarray(lane_nodes()))
 

time: 22.8 us -> 21.6 us (0.947)
  Pallas kernels: 4.33 us -> 3.1 us
    pallas_call x1, Pallas kernels: 4.33 us -> 3.1 us  [run_levels(): pl.pallas_call(functools.partial(kernel, plan, row_bits, ('outer', 'inner...]
where the time goes in v2:
time: 21.6 us; the launch traced here: 21.4 us
  blocking collectives  18.3 us (85%)
  Pallas kernels  3.1 us (14%)
    all_to_all x1, blocking collectives, body(): rows = lax.all_to_all(weights, ('inner', 'outer'), 0, 0, tiled=True)  18.3 us
    pallas_call x1, Pallas kernels, run_levels(): pl.pallas_call(functools.partial(kernel, plan, row_bits, ('outer', 'inner...  3.1 us

profile of v2, /device:TPU:0, one launch (start us, length us, event | category | flops | bytes accessed | tf_op | source)
XLA Modules:
  0.0 21.4 jit_solution(854714765088965360)
XLA Ops:
  0.0 0.0 copy-start
  0.0 0.0 copy-start.1
  0.0 18.3 %all_to_all.11 = f32[32,16,128]{2,1,0:T(8,128)S(1)} all-to-all(f32[32,16,128]{2,1,0:T(8,128)} %bitcast.3), channel_id=1, replica_groups=mesh['outer'=4,'inner'=8] {'inner','outer'}, dimensions={0} | all-to-all | bytes 524288 | tf_op jit(solution)/shard_map/all_to_all | solution.py:430
  18.3 0.0 copy-done
  18.3 0.0 copy-done.1
  18.3 3.1 %shard_map.37 = f32[512,128]{1,0:T(8,128)} custom-call(f32[512,128]{1,0:T(8,128)S(1)} %bitcast.2, bf16[2,256,256]{2,1,0:T(8,128)(2,1)S(1)} %copy-done, f32[8,128]{1,0:T(8,128)S(1)} %copy-done.1), custom_call_target="tpu_custom_call" | custom-call | tf_op jit(solution)/shard_map/pallas_call | solution.py:397
Async XLA Ops:
  0.0 18.3 %copy-start = (bf16[2,256,256]{2,1,0:T(8,128)(2,1)S(1)}, bf16[2,256,256]{2,1,0:T(8,128)(2,1)}, u32[]{:S(2)}) copy-start(bf16[2,256,256]{2,1,0:T(8,128)(2,1)} %constant.4.clone.matrix_ref) | copy-start | bytes 786436
  0.0 18.3 %copy-start.1 = (f32[8,128]{1,0:T(8,128)S(1)}, f32[8,128]{1,0:T(8,128)}, u32[]{:S(2)}) copy-start(f32[8,128]{1,0:T(8,128)} %constant.5.clone.node_ref) | copy-start | bytes 12292

commit v3 on v2

v3 whole, which is shorter than its diff:
```python
import functools

import jax
import jax.numpy as jnp
import numpy as np
from jax import lax
from jax.experimental import pallas as pl
from jax.experimental.pallas import tpu as pltpu
from jax.sharding import PartitionSpec as P

GRID_N = 16384
TREE_LEVELS = 11
LOW_BITS = 4
BLOCK = 1 << LOW_BITS
VMEM_BYTES = 16 * 1024 * 1024
DOTS = 2


def chebyshev_nodes():
    return 0.5 * np.cos(np.pi * (2.0 * np.arange(8) + 1.0) / 16.0)


def lagrange_weights(which_child):
    node_values = chebyshev_nodes()
    targets = (node_values + which_child - 0.5) / 2.0
    weights_table = np.ones((8, 8))
    for anchor in range(8):
        for other_node in range(8):
            if other_node != anchor:
                weights_table[anchor, :] = (
                    weights_table[anchor, :]
                    * (targets - node_values[other_node])
                    / (node_values[anchor] - node_values[other_node])
                )
    return weights_table


def merge_matrix(dimension):
    merge_table = np.zeros((256, 128))
    for which_child in range(2):
        weights_table = lagrange_weights(which_child)
        if dimension == 0:
            block_table = np.kron(weights_table, np.eye(8))
        else:
            block_table = np.kron(np.eye(8), weights_table)
        for half in range(2):
            first = half * 128 + which_child * 64
            merge_table[first : first + 64, half * 64 : half * 64 + 64] = block_table.T
    return merge_table


def split_matrices():
    parts = []
    for dimension in range(2):
        exact = merge_matrix(dimension).astype(np.float32)
        high = exact.astype(jnp.bfloat16)
        low = (exact - high.astype(np.float32)).astype(jnp.bfloat16)
        parts.append(np.concatenate([high, low], 1))
    return np.stack(parts)


def lane_nodes():
    lanes = np.arange(128) % 64
    nodes = chebyshev_nodes()
    return np.stack([nodes[lanes // 8], nodes[lanes % 8]] + [np.zeros(128)] * 6).astype(np.float32)


def level_plan(local_bits, inner_bits, outer_bits):
    levels_total = inner_bits + outer_bits
    carried = [local_bits + level for level in range(levels_total)]
    moved = [
        local_bits - inner_bits + level
        if level < inner_bits
        else local_bits - levels_total + level - inner_bits
        for level in range(levels_total)
    ]
    source = [[], []]
    for level in range(levels_total):
        source[(level + 1) % 2].append(("carried", level))
    source[0] += [local_bits - 7, local_bits - 6, local_bits - 5]
    source[1] += [local_bits - 4, local_bits - 3, local_bits - 2, local_bits - 1]
    target = [[], []]
    for ordinal in range(local_bits - 7):
        target[ordinal % 2].append(ordinal)

    def place(bit):
        if isinstance(bit, tuple):
            return moved[bit[1]]
        if bit in moved:
            return (moved.index(bit),)
        return bit

    source = [[place(bit) for bit in group] for group in source]
    target = [[place(bit) for bit in group] for group in target]
    plan = []
    for level in range(levels_total):
        dimension = (level + 1) % 2
        plan.append(
            (dimension, moved[level], [list(g) for g in target], [list(g) for g in source])
        )
        source[dimension] = source[dimension][1:]
        target[dimension] = [moved[level]] + target[dimension]
    plan.append((None, None, [list(g) for g in target], [list(g) for g in source]))
    return plan


def box_span(source):
    return GRID_N * 2.0 ** (len(source) - TREE_LEVELS)


def reduced(turns):
    return turns - jnp.floor(turns + 0.5)


def odd_series(coefficients, near, square):
    total = coefficients[-1]
    for coefficient in coefficients[-2::-1]:
        total = total * square + coefficient
    return total * near


def sincos(turns):
    near = turns - lax.round(turns, lax.RoundingMethod.TO_NEAREST_EVEN)
    square = near * near
    sine = series(SINE, square) * near
    cosine = series(COSINE, square)
    return sine * cosine, 1.0 - sine * sine


def series(coefficients, square):
    total = coefficients[-1]
    for coefficient in coefficients[-2::-1]:
        total = total * square + coefficient
    return total


def fit(function, powers):
    grid = 0.25 * (1.0 - np.cos(np.pi * (np.arange(2000) + 0.5) / 2000))
    matrix = np.stack([grid**power for power in powers], 1)
    exact = np.sqrt(2.0) * function(np.pi * grid)
    weight = np.ones_like(grid)
    best = None
    for _ in range(100):
        scale = np.sqrt(weight)
        solved = np.linalg.lstsq(matrix * scale[:, None], exact * scale, rcond=None)[0]
        error = np.abs(matrix @ solved - exact)
        if best is None or error.max() < best[0]:
            best = (error.max(), solved)
        weight = weight * error
        weight = weight / weight.sum()
    return [float(v) for v in best[1]]


SINE = fit(np.sin, (1, 3, 5, 7, 9))
COSINE = fit(np.cos, (0, 2, 4, 6, 8))


def combos(bits):
    result = [{}]
    for bit in bits:
        result = [{**one, bit: value} for one in result for value in range(2)]
    return result


def pick(assignment, bits):
    return tuple(assignment[bit] for bit in bits)


class Layout:
    def __init__(self, plan, row_bits):
        self.plan = plan
        self.leading = list(range(row_bits - 1, LOW_BITS - 1, -1))
        self.moved = [entry[1] for entry in plan[:-1]]
        self.packed = self.moved + [[bit for bit in self.leading if bit != self.moved[-1]][0]]
        self.entries = {}
        for level, packed in enumerate(self.packed):
            free = self.free(level)
            for one in combos(free):
                for branch in range(2 if level < len(self.moved) else 1):
                    self.entries[level, pick(one, free), branch] = len(self.entries)

    def free(self, level):
        return [bit for bit in self.leading if bit != self.packed[level]]

    def place(self, level, one, branch=0):
        first = self.entries[level, pick(one, self.free(level)), branch] * 2 * BLOCK
        return slice(first, first + BLOCK), slice(first + BLOCK, first + 2 * BLOCK)

    def row(self, assignment):
        return sum(assignment[bit] << bit for bit in self.leading if bit in assignment)


def table_kernel(layout, axes, node_ref, table_ref):
    plan = layout.plan
    device = lax.axis_index(axes[0]) * lax.axis_size(axes[1]) + lax.axis_index(axes[1])
    rows = lax.broadcasted_iota(jnp.int32, (BLOCK, 128), 0)
    lanes = lax.broadcasted_iota(jnp.int32, (BLOCK, 128), 1)
    half = jnp.where(lanes < 64, 0.0, 1.0)
    row_bit = [(rows >> bit & 1).astype(jnp.float32) for bit in range(LOW_BITS)]
    node = [jnp.broadcast_to(node_ref[d : d + 1, :], (BLOCK, 128)) for d in range(2)]

    def index_tile(places, packed):
        total = jnp.full((BLOCK, 128), 0.5, jnp.float32)
        scalar = None
        for ordinal, where in enumerate(places):
            weight = float(1 << ordinal)
            if isinstance(where, tuple):
                term = (device >> where[0] & 1).astype(jnp.float32) * weight
                scalar = term if scalar is None else scalar + term
            elif where == packed:
                total = total + half * weight
            elif where < LOW_BITS:
                total = total + row_bit[where] * weight
        return total if scalar is None else total + scalar

    def index_lead(places, assignment):
        return sum(
            float(1 << ordinal) * assignment[where]
            for ordinal, where in enumerate(places)
            if not isinstance(where, tuple) and where in assignment
        )

    def by_lead(places, level, function):
        bits = [w for w in places if not isinstance(w, tuple) and w in layout.free(level)]
        tile = index_tile(places, layout.packed[level])
        values = {pick(one, bits): function(tile + index_lead(places, one)) for one in combos(bits)}
        return lambda one: values[pick(one, bits)]

    def root(value):
        return value * lax.rsqrt(value)

    def store(level, one, branch, turns):
        sine, cosine = sincos(turns)
        for place, value in zip(layout.place(level, one, branch), (cosine, sine)):
            table_ref[place, :] = value

    for level, (dimension, _, target, source) in enumerate(plan):
        width = [2.0 ** (-len(source[d])) for d in range(2)]
        span = [box_span(source[d]) for d in range(2)]
        waves = [
            by_lead(source[d], level, lambda box, d=d: sincos((box + node[d]) * width[d]))
            for d in range(2)
        ]
        center = [
            by_lead(target[d], level, lambda box, d=d: box * span[d] - GRID_N / 2.0)
            for d in range(2)
        ]
        for one in combos(layout.free(level)):
            (sine_one, cosine_one), (sine_two, cosine_two) = (waves[d](one) for d in range(2))
            speed = [0.125 + sine_one * sine_two * 0.0625, 0.125 + cosine_one * cosine_two * 0.0625]
            square = [value * value for value in speed]
            k = [center[d](one) for d in range(2)]
            if level == len(plan) - 1:
                radius = root(square[0] * (k[0] * k[0]) + square[1] * (k[1] * k[1]))
                linear = node[0] * width[0] * k[0] + node[1] * width[1] * k[1]
                store(level, one, 0, (radius - jnp.floor(radius)) + linear)
                continue
            other = 1 - dimension
            fixed = square[other] * (k[other] * k[other])
            radius = root(fixed + square[dimension] * (k[dimension] * k[dimension]))
            for branch in range(2):
                shift = (branch - 0.5) * 0.5 * span[dimension]
                child = k[dimension] + shift
                turns = root(fixed + square[dimension] * (child * child))
                if level > 0:
                    turns = (turns - radius) + node[dimension] * (width[dimension] * shift)
                else:
                    linear = node[dimension] * width[dimension] * child
                    linear = linear + node[other] * width[other] * k[other]
                    turns = (turns - jnp.floor(turns)) + linear
                store(level, one, branch, turns)


def level_kernel(layout, x_ref, table_ref, matrix_ref, out_ref, done_ref, sems):
    low_half = lax.broadcasted_iota(jnp.int32, (BLOCK, 128), 1) < 64
    last = len(layout.moved)

    def pack(first, second):
        return (
            jnp.where(low_half, first, pltpu.roll(second, 64, 1)),
            jnp.where(low_half, pltpu.roll(first, 64, 1), second),
        )

    state = {}
    for one in combos(layout.free(0)):
        halves = []
        for value in range(2):
            first = layout.row({**one, layout.packed[0]: value})
            halves.append(x_ref[first : first + BLOCK, :])
        state[pick(one, layout.free(0))] = pack(*halves)

    for level, moved in enumerate(layout.moved):
        free, packed = layout.free(level), layout.packed[level + 1]
        next_free = layout.free(level + 1)
        matrix = matrix_ref[layout.plan[level][0]]
        later = layout.packed[level + 1 :]
        order = sorted(
            (bit for bit in next_free if bit != moved),
            key=lambda bit: -later.index(bit) if bit in later else 0,
        )
        next_state = {}
        groups = combos(order)
        step = max(1, len(groups) // DOTS)
        for start in range(0, len(groups), step):
            parts = ([], [])
            places = []
            for group in groups[start : start + step]:
                halves = []
                for half in range(2):
                    one = {**group, packed: half}
                    real, imaginary = state[pick(one, free)]
                    turned = []
                    for branch in range(2):
                        cosine, sine = (table_ref[place, :] for place in layout.place(level, one, branch))
                        turned += [real * cosine - imaginary * sine, real * sine + imaginary * cosine]
                    halves.append(turned)
                for index in range(4):
                    value = jnp.concatenate([turned[index] for turned in halves], 1)
                    top = value.astype(jnp.bfloat16)
                    parts[0].append(top)
                    parts[1].append((value - top.astype(jnp.float32)).astype(jnp.bfloat16))
                places += [pick({**group, moved: branch}, next_free) for branch in range(2)]
            total = sum(
                jnp.dot(jnp.concatenate(part, 0), matrix, preferred_element_type=jnp.float32)
                for part in parts
            )
            total = total[:, :128] + total[:, 128:]
            for index, place in enumerate(places):
                first = 2 * index * BLOCK
                next_state[place] = (
                    total[first : first + BLOCK],
                    total[first + BLOCK : first + 2 * BLOCK],
                )
        state = next_state

    packed, free = layout.packed[last], layout.free(last)
    copies = []
    for one in combos(free):
        real, imaginary = state[pick(one, free)]
        cosine, sine = (table_ref[place, :] for place in layout.place(last, one))
        outputs = pack(real * cosine + imaginary * sine, imaginary * cosine - real * sine)
        for value in range(2):
            first = layout.row({**one, packed: value})
            done_ref[first : first + BLOCK, :] = outputs[value]
        if all(one[bit] == 1 for bit in free[2:]):
            for value in range(2):
                shared = {bit: one[bit] for bit in free[:2]}
                piece = pl.ds(layout.row({**shared, packed: value}), BLOCK << len(free) - 2)
                copy = pltpu.make_async_copy(done_ref.at[piece], out_ref.at[piece], sems.at[len(copies)])
                copy.start()
                copies.append(copy)
    for copy in copies:
        copy.wait()


def rotations(layout):
    vmem = pl.BlockSpec(memory_space=pltpu.VMEM)
    rows = 2 * BLOCK * len(layout.entries)
    return pl.pallas_call(
        functools.partial(table_kernel, layout, ("outer", "inner")),
        out_shape=jax.ShapeDtypeStruct((rows, 128), jnp.float32),
        in_specs=[vmem],
        out_specs=vmem,
        compiler_params=pltpu.CompilerParams(vmem_limit_bytes=VMEM_BYTES),
        cost_estimate=pl.CostEstimate(
            flops=rows * 128 * 20, bytes_accessed=rows * 512, transcendentals=rows * 128
        ),
    )(jnp.asarray(lane_nodes()))


def run_levels(rows, table, layout):
    vmem = pl.BlockSpec(memory_space=pltpu.VMEM)
    return pl.pallas_call(
        functools.partial(level_kernel, layout),
        out_shape=jax.ShapeDtypeStruct(rows.shape, jnp.float32),
        in_specs=[vmem] * 3,
        out_specs=pl.BlockSpec(memory_space=pl.ANY),
        scratch_shapes=[pltpu.VMEM(rows.shape, jnp.float32), pltpu.SemaphoreType.DMA((8,))],
        compiler_params=pltpu.CompilerParams(vmem_limit_bytes=VMEM_BYTES),
    )(rows, table, jnp.asarray(split_matrices()))


def reorder_plan(plan, order):
    def place(bit):
        return bit if bit is None or isinstance(bit, tuple) else order.index(bit)

    return [
        (dimension, place(moved), [[place(b) for b in g] for g in target], [[place(b) for b in g] for g in source])
        for dimension, moved, target, source in plan
    ]


def reorder_rows(rows, order):
    count = len(order)
    if list(order) == list(range(count)):
        return rows
    axes = [count - 1 - order[count - 1 - i] for i in range(count)]
    return rows.reshape((2,) * count + (128,)).transpose(axes + [count]).reshape(rows.shape)


def level_groups(plan, row_bits):
    moved = [entry[1] for entry in plan[:-1]]
    groups = []
    level = 0
    while level < len(moved):
        count = min(len(moved) - level, row_bits - LOW_BITS)
        group = moved[level : level + count]
        order = [bit for bit in range(row_bits) if bit not in group] + sorted(group)
        groups.append((order, Layout(reorder_plan(plan[level : level + count + 1], order), row_bits)))
        level += count
    return groups


def body(weights):
    row_bits = weights.shape[0].bit_length() - 1
    inner_bits = lax.axis_size("inner").bit_length() - 1
    outer_bits = lax.axis_size("outer").bit_length() - 1
    groups = level_groups(level_plan(row_bits, inner_bits, outer_bits), row_bits)
    rows = lax.all_to_all(weights, ("inner", "outer"), 0, 0, tiled=True)
    tables = [rotations(layout) for _, layout in groups]
    for (order, layout), table in zip(groups, tables):
        rows = run_levels(reorder_rows(rows, order), table, layout)
        rows = reorder_rows(rows, [order.index(bit) for bit in range(row_bits)])
    return rows


def solution(mesh):
    spec = P(("outer", "inner"), None)
    return jax.shard_map(body, mesh=mesh, in_specs=(spec,), out_specs=spec, check_vma=False)
```

time: 21.6 us -> 20.7 us (0.958)
  blocking collectives: 18.3 us -> 0 us
  waiting for transfers between devices: 0 us -> 8.55 us
  starting transfers between devices: 0 us -> 7.3 us
  Pallas kernels: 3.1 us -> 3.9 us
  local copies, waits for them, and re-layouts: 0.01 us -> 0.69 us
    all_to_all x1 -> x0, blocking collectives: 18.3 us -> none  [body(): rows = lax.all_to_all(weights, ('inner', 'outer'), 0, 0, tiled=True)]
    all_to_all x0 -> x1, waiting for transfers between devices: none -> 8.55 us  [body(): rows = lax.all_to_all(weights, ('inner', 'outer'), 0, 0, tiled=True)]
    all_to_all x0 -> x1, starting transfers between devices: none -> 7.3 us  [body(): rows = lax.all_to_all(weights, ('inner', 'outer'), 0, 0, tiled=True)]
    pallas_call x1 -> x2, Pallas kernels: 3.1 us -> 3.9 us  [the longest x1 2.2 us: run_levels(): pl.pallas_call(functools.partial(level_kernel, layout), out_shape=jax.Sha...]
    unnamed x4, local copies, waits for them, and re-layouts: 0.01 us -> 0.69 us
  transfers between devices with their start and end apart: 0 -> 1, of which waited for: 0 -> 1; matrix products, arithmetic and copies ran while one was open for 0% -> 0% of each run, Pallas kernels for 0% -> 8%
where the time goes in v3:
time: 20.7 us; the launch traced here: 20.5 us
  waiting for transfers between devices  8.55 us (41%)
  starting transfers between devices  7.3 us (35%)
  Pallas kernels  3.9 us (19%)
  local copies, waits for them, and re-layouts  0.69 us (3%)
    all_to_all x1, waiting for transfers between devices, body(): rows = lax.all_to_all(weights, ('inner', 'outer'), 0, 0, tiled=True)  8.55 us
    all_to_all x1, starting transfers between devices, body(): rows = lax.all_to_all(weights, ('inner', 'outer'), 0, 0, tiled=True)  7.3 us
    pallas_call x1, Pallas kernels, run_levels(): pl.pallas_call(functools.partial(level_kernel, layout), out_shape=jax.Sha...  2.2 us
    pallas_call x1, Pallas kernels, rotations(): pl.pallas_call(functools.partial(table_kernel, layout, ('outer', 'inner')...  1.7 us
    unnamed x4, local copies, waits for them, and re-layouts  0.69 us
  transfers between devices with their start and end apart: 1, of which 1 were waited for; matrix products, arithmetic and copies ran while one was open for 0% of the time, Pallas kernels for 8%

profile of v3, /device:TPU:0, one launch (start us, length us, event | category | flops | bytes accessed | tf_op | source)
XLA Modules:
  0.0 20.5 jit_solution(5414167877936998243)
XLA Ops:
  0.0 0.0 copy-start
  0.0 7.3 %all-to-all-start = ((f32[32,16,128]{2,1,0:T(8,128)}), f32[32,16,128]{2,1,0:T(8,128)S(1)}, u32[]{:S(2)}, u32[]{:S(2)}) async-start(f32[32,16,128]{2,1,0:T(8,128)} %bitcast.3), calls=%async_computation | async-start | bytes 524288 | tf_op jit(solution)/shard_map/all_to_all | solution.py:419
  7.3 0.0 copy-start.1
  7.3 0.7 %copy-done.1 = f32[8,128]{1,0:T(8,128)S(1)} copy-done((f32[8,128]{1,0:T(8,128)S(1)}, f32[8,128]{1,0:T(8,128)}, u32[]{:S(2)}) %copy-start.1) | copy-done | bytes 4120
  8.0 1.7 %shard_map.37.table_ref = f32[5632,128]{1,0:T(8,128)S(1)} custom-call(f32[8,128]{1,0:T(8,128)S(1)} %copy-done.1), custom_call_target="tpu_custom_call" | custom-call | flops 14417920 | bytes 2883584 | tf_op jit(solution)/shard_map/pallas_call | solution.py:359
  9.7 8.6 %all-to-all-done = f32[32,16,128]{2,1,0:T(8,128)S(1)} async-done(((f32[32,16,128]{2,1,0:T(8,128)}), f32[32,16,128]{2,1,0:T(8,128)S(1)}, u32[]{:S(2)}, u32[]{:S(2)}) %all-to-all-start) | async-done | bytes 262176 | tf_op jit(solution)/shard_map/all_to_all | solution.py:419
  18.3 0.0 copy-done
  18.3 2.2 %shard_map.38 = f32[512,128]{1,0:T(8,128)} custom-call(f32[512,128]{1,0:T(8,128)S(1)} %bitcast.2, f32[5632,128]{1,0:T(8,128)S(1)} %shard_map.37.table_ref, bf16[2,256,256]{2,1,0:T(8,128)(2,1)S(1)} %copy-done), custom_call_target="tpu_custom_call" | custom-call | tf_op jit(solution)/shard_map/pallas_call | solution.py:373
Async XLA Ops:
  0.0 18.3 %copy-start = (bf16[2,256,256]{2,1,0:T(8,128)(2,1)S(1)}, bf16[2,256,256]{2,1,0:T(8,128)(2,1)}, u32[]{:S(2)}) copy-start(bf16[2,256,256]{2,1,0:T(8,128)(2,1)} %constant.5.clone.matrix_ref) | copy-start | bytes 786436
  0.0 18.3 %all-to-all-start = ((f32[32,16,128]{2,1,0:T(8,128)}), f32[32,16,128]{2,1,0:T(8,128)S(1)}, u32[]{:S(2)}, u32[]{:S(2)}) async-start(f32[32,16,128]{2,1,0:T(8,128)} %bitcast.3), calls=%async_computation | async-start | bytes 524288 | tf_op jit(solution)/shard_map/all_to_all | solution.py:419
  7.3 0.7 %copy-start.1 = (f32[8,128]{1,0:T(8,128)S(1)}, f32[8,128]{1,0:T(8,128)}, u32[]{:S(2)}) copy-start(f32[8,128]{1,0:T(8,128)} %constant.4.clone.node_ref) | copy-start | bytes 12292

commit v4 on v3

--- a/solution.py
+++ b/solution.py
@@ -302,7 +302,7 @@
         groups = combos(order)
         step = max(1, len(groups) // DOTS)
         for start in range(0, len(groups), step):
-            parts = ([], [])
+            parts = []
             places = []
             for group in groups[start : start + step]:
                 halves = []
@@ -314,23 +314,23 @@
                         cosine, sine = (table_ref[place, :] for place in layout.place(level, one, branch))
                         turned += [real * cosine - imaginary * sine, real * sine + imaginary * cosine]
                     halves.append(turned)
-                for index in range(4):
-                    value = jnp.concatenate([turned[index] for turned in halves], 1)
-                    top = value.astype(jnp.bfloat16)
-                    parts[0].append(top)
-                    parts[1].append((value - top.astype(jnp.float32)).astype(jnp.bfloat16))
+                values = [jnp.concatenate([turned[index] for turned in halves], 1) for index in range(4)]
+                tops = [value.astype(jnp.bfloat16) for value in values]
+                parts += tops
+                parts += [
+                    (value - top.astype(jnp.float32)).astype(jnp.bfloat16)
+                    for value, top in zip(values, tops)
+                ]
                 places += [pick({**group, moved: branch}, next_free) for branch in range(2)]
-            total = sum(
-                jnp.dot(jnp.concatenate(part, 0), matrix, preferred_element_type=jnp.float32)
-                for part in parts
-            )
-            total = total[:, :128] + total[:, 128:]
+            product = jnp.dot(jnp.concatenate(parts, 0), matrix, preferred_element_type=jnp.float32)
             for index, place in enumerate(places):
-                first = 2 * index * BLOCK
-                next_state[place] = (
-                    total[first : first + BLOCK],
-                    total[first + BLOCK : first + 2 * BLOCK],
-                )
+                first = (index // 2 * 8 + index % 2 * 2) * BLOCK
+                pair = []
+                for component in range(2):
+                    top = product[first + component * BLOCK : first + (component + 1) * BLOCK]
+                    rest = product[first + (component + 4) * BLOCK : first + (component + 5) * BLOCK]
+                    pair.append((top[:, 128:] + rest[:, :128]) + top[:, :128])
+                next_state[place] = pair
         state = next_state
 
     packed, free = layout.packed[last], layout.free(last)

time: 20.7 us -> 20.5 us (level)
  Pallas kernels: 3.9 us -> 3.67 us
    pallas_call x1, Pallas kernels: 2.2 us -> 1.97 us  [run_levels(): pl.pallas_call(functools.partial(level_kernel, layout), out_shape=jax.Sha...]
where the time goes in v4:
time: 20.5 us; the launch traced here: 20.2 us
  waiting for transfers between devices  8.55 us (42%)
  starting transfers between devices  7.3 us (36%)
  Pallas kernels  3.67 us (18%)
  local copies, waits for them, and re-layouts  0.69 us (3%)
    all_to_all x1, waiting for transfers between devices, body(): rows = lax.all_to_all(weights, ('inner', 'outer'), 0, 0, tiled=True)  8.55 us
    all_to_all x1, starting transfers between devices, body(): rows = lax.all_to_all(weights, ('inner', 'outer'), 0, 0, tiled=True)  7.3 us
    pallas_call x1, Pallas kernels, run_levels(): pl.pallas_call(functools.partial(level_kernel, layout), out_shape=jax.Sha...  1.97 us
    pallas_call x1, Pallas kernels, rotations(): pl.pallas_call(functools.partial(table_kernel, layout, ('outer', 'inner')...  1.7 us
    unnamed x4, local copies, waits for them, and re-layouts  0.69 us
  transfers between devices with their start and end apart: 1, of which 1 were waited for; matrix products, arithmetic and copies ran while one was open for 0% of the time, Pallas kernels for 8%

profile of v4, /device:TPU:0, one launch (start us, length us, event | category | flops | bytes accessed | tf_op | source)
XLA Modules:
  0.0 20.2 jit_solution(15767800622640423681)
XLA Ops:
  0.0 0.0 copy-start
  0.0 7.3 %all-to-all-start = ((f32[32,16,128]{2,1,0:T(8,128)}), f32[32,16,128]{2,1,0:T(8,128)S(1)}, u32[]{:S(2)}, u32[]{:S(2)}) async-start(f32[32,16,128]{2,1,0:T(8,128)} %bitcast.3), calls=%async_computation | async-start | bytes 524288 | tf_op jit(solution)/shard_map/all_to_all | solution.py:419
  7.3 0.0 copy-start.1
  7.3 0.7 %copy-done.1 = f32[8,128]{1,0:T(8,128)S(1)} copy-done((f32[8,128]{1,0:T(8,128)S(1)}, f32[8,128]{1,0:T(8,128)}, u32[]{:S(2)}) %copy-start.1) | copy-done | bytes 4120
  8.0 1.7 %shard_map.37.table_ref = f32[5632,128]{1,0:T(8,128)S(1)} custom-call(f32[8,128]{1,0:T(8,128)S(1)} %copy-done.1), custom_call_target="tpu_custom_call" | custom-call | flops 14417920 | bytes 2883584 | tf_op jit(solution)/shard_map/pallas_call | solution.py:359
  9.7 8.6 %all-to-all-done = f32[32,16,128]{2,1,0:T(8,128)S(1)} async-done(((f32[32,16,128]{2,1,0:T(8,128)}), f32[32,16,128]{2,1,0:T(8,128)S(1)}, u32[]{:S(2)}, u32[]{:S(2)}) %all-to-all-start) | async-done | bytes 262176 | tf_op jit(solution)/shard_map/all_to_all | solution.py:419
  18.3 0.0 copy-done
  18.3 2.0 %shard_map.38 = f32[512,128]{1,0:T(8,128)} custom-call(f32[512,128]{1,0:T(8,128)S(1)} %bitcast.2, f32[5632,128]{1,0:T(8,128)S(1)} %shard_map.37.table_ref, bf16[2,256,256]{2,1,0:T(8,128)(2,1)S(1)} %copy-done), custom_call_target="tpu_custom_call" | custom-call | tf_op jit(solution)/shard_map/pallas_call | solution.py:373
Async XLA Ops:
  0.0 18.3 %copy-start = (bf16[2,256,256]{2,1,0:T(8,128)(2,1)S(1)}, bf16[2,256,256]{2,1,0:T(8,128)(2,1)}, u32[]{:S(2)}) copy-start(bf16[2,256,256]{2,1,0:T(8,128)(2,1)} %constant.5.clone.matrix_ref) | copy-start | bytes 786436
  0.0 18.3 %all-to-all-start = ((f32[32,16,128]{2,1,0:T(8,128)}), f32[32,16,128]{2,1,0:T(8,128)S(1)}, u32[]{:S(2)}, u32[]{:S(2)}) async-start(f32[32,16,128]{2,1,0:T(8,128)} %bitcast.3), calls=%async_computation | async-start | bytes 524288 | tf_op jit(solution)/shard_map/all_to_all | solution.py:419
  7.3 0.7 %copy-start.1 = (f32[8,128]{1,0:T(8,128)S(1)}, f32[8,128]{1,0:T(8,128)}, u32[]{:S(2)}) copy-start(f32[8,128]{1,0:T(8,128)} %constant.4.clone.node_ref) | copy-start | bytes 12292

commit v5 on v4

--- a/solution.py
+++ b/solution.py
@@ -10,10 +10,10 @@
 
 GRID_N = 16384
 TREE_LEVELS = 11
-LOW_BITS = 4
+LOW_BITS = 3
 BLOCK = 1 << LOW_BITS
 VMEM_BYTES = 16 * 1024 * 1024
-DOTS = 2
+DOTS = 4
 
 
 def chebyshev_nodes():
@@ -296,7 +296,7 @@
         later = layout.packed[level + 1 :]
         order = sorted(
             (bit for bit in next_free if bit != moved),
-            key=lambda bit: -later.index(bit) if bit in later else 0,
+            key=lambda bit: -later.index(bit) if bit in later else -99 * (bit not in layout.packed),
         )
         next_state = {}
         groups = combos(order)
@@ -312,9 +312,10 @@
                     turned = []
                     for branch in range(2):
                         cosine, sine = (table_ref[place, :] for place in layout.place(level, one, branch))
-                        turned += [real * cosine - imaginary * sine, real * sine + imaginary * cosine]
+                        both = (real * cosine - imaginary * sine, real * sine + imaginary * cosine)
+                        turned.append(jnp.concatenate(both, 0))
                     halves.append(turned)
-                values = [jnp.concatenate([turned[index] for turned in halves], 1) for index in range(4)]
+                values = [jnp.concatenate([turned[branch] for turned in halves], 1) for branch in range(2)]
                 tops = [value.astype(jnp.bfloat16) for value in values]
                 parts += tops
                 parts += [
@@ -324,13 +325,11 @@
                 places += [pick({**group, moved: branch}, next_free) for branch in range(2)]
             product = jnp.dot(jnp.concatenate(parts, 0), matrix, preferred_element_type=jnp.float32)
             for index, place in enumerate(places):
-                first = (index // 2 * 8 + index % 2 * 2) * BLOCK
-                pair = []
-                for component in range(2):
-                    top = product[first + component * BLOCK : first + (component + 1) * BLOCK]
-                    rest = product[first + (component + 4) * BLOCK : first + (component + 5) * BLOCK]
-                    pair.append((top[:, 128:] + rest[:, :128]) + top[:, :128])
-                next_state[place] = pair
+                first = (index // 2 * 4 + index % 2) * 2 * BLOCK
+                top = product[first : first + 2 * BLOCK]
+                rest = product[first + 4 * BLOCK : first + 6 * BLOCK]
+                total = (top[:, 128:] + rest[:, :128]) + top[:, :128]
+                next_state[place] = (total[:BLOCK], total[BLOCK:])
         state = next_state
 
     packed, free = layout.packed[last], layout.free(last)

time: 20.5 us -> 20.3 us (level)
  no operation moved by 1% of the time
where the time goes in v5:
time: 20.3 us; the launch traced here: 20 us
  waiting for transfers between devices  8.58 us (42%)
  starting transfers between devices  7.3 us (36%)
  Pallas kernels  3.47 us (17%)
  local copies, waits for them, and re-layouts  0.69 us (3%)
    all_to_all x1, waiting for transfers between devices, body(): rows = lax.all_to_all(weights, ('inner', 'outer'), 0, 0, tiled=True)  8.58 us
    all_to_all x1, starting transfers between devices, body(): rows = lax.all_to_all(weights, ('inner', 'outer'), 0, 0, tiled=True)  7.3 us
    pallas_call x1, Pallas kernels, run_levels(): pl.pallas_call(functools.partial(level_kernel, layout), out_shape=jax.Sha...  1.79 us
    pallas_call x1, Pallas kernels, rotations(): pl.pallas_call(functools.partial(table_kernel, layout, ('outer', 'inner')...  1.68 us
    unnamed x4, local copies, waits for them, and re-layouts  0.69 us
  transfers between devices with their start and end apart: 1, of which 1 were waited for; matrix products, arithmetic and copies ran while one was open for 0% of the time, Pallas kernels for 8%

profile of v5, /device:TPU:0, one launch (start us, length us, event | category | flops | bytes accessed | tf_op | source)
XLA Modules:
  0.0 20.0 jit_solution(9766058224238336604)
XLA Ops:
  0.0 0.0 copy-start
  0.0 7.3 %all-to-all-start = ((f32[32,16,128]{2,1,0:T(8,128)}), f32[32,16,128]{2,1,0:T(8,128)S(1)}, u32[]{:S(2)}, u32[]{:S(2)}) async-start(f32[32,16,128]{2,1,0:T(8,128)} %bitcast.3), calls=%async_computation | async-start | bytes 524288 | tf_op jit(solution)/shard_map/all_to_all | solution.py:418
  7.3 0.0 copy-start.1
  7.3 0.7 %copy-done.1 = f32[8,128]{1,0:T(8,128)S(1)} copy-done((f32[8,128]{1,0:T(8,128)S(1)}, f32[8,128]{1,0:T(8,128)}, u32[]{:S(2)}) %copy-start.1) | copy-done | bytes 4120
  8.0 1.7 %shard_map.37.table_ref = f32[5632,128]{1,0:T(8,128)S(1)} custom-call(f32[8,128]{1,0:T(8,128)S(1)} %copy-done.1), custom_call_target="tpu_custom_call" | custom-call | flops 14417920 | bytes 2883584 | tf_op jit(solution)/shard_map/pallas_call | solution.py:358
  9.7 8.6 %all-to-all-done = f32[32,16,128]{2,1,0:T(8,128)S(1)} async-done(((f32[32,16,128]{2,1,0:T(8,128)}), f32[32,16,128]{2,1,0:T(8,128)S(1)}, u32[]{:S(2)}, u32[]{:S(2)}) %all-to-all-start) | async-done | bytes 262176 | tf_op jit(solution)/shard_map/all_to_all | solution.py:418
  18.3 0.0 copy-done
  18.3 1.8 %shard_map.38 = f32[512,128]{1,0:T(8,128)} custom-call(f32[512,128]{1,0:T(8,128)S(1)} %bitcast.2, f32[5632,128]{1,0:T(8,128)S(1)} %shard_map.37.table_ref, bf16[2,256,256]{2,1,0:T(8,128)(2,1)S(1)} %copy-done), custom_call_target="tpu_custom_call" | custom-call | tf_op jit(solution)/shard_map/pallas_call | solution.py:372
Async XLA Ops:
  0.0 18.3 %copy-start = (bf16[2,256,256]{2,1,0:T(8,128)(2,1)S(1)}, bf16[2,256,256]{2,1,0:T(8,128)(2,1)}, u32[]{:S(2)}) copy-start(bf16[2,256,256]{2,1,0:T(8,128)(2,1)} %constant.5.clone.matrix_ref) | copy-start | bytes 786436
  0.0 18.3 %all-to-all-start = ((f32[32,16,128]{2,1,0:T(8,128)}), f32[32,16,128]{2,1,0:T(8,128)S(1)}, u32[]{:S(2)}, u32[]{:S(2)}) async-start(f32[32,16,128]{2,1,0:T(8,128)} %bitcast.3), calls=%async_computation | async-start | bytes 524288 | tf_op jit(solution)/shard_map/all_to_all | solution.py:418
  7.3 0.7 %copy-start.1 = (f32[8,128]{1,0:T(8,128)S(1)}, f32[8,128]{1,0:T(8,128)}, u32[]{:S(2)}) copy-start(f32[8,128]{1,0:T(8,128)} %constant.4.clone.node_ref) | copy-start | bytes 12292

commit v6 on v5

--- a/solution.py
+++ b/solution.py
@@ -171,19 +171,21 @@
         self.plan = plan
         self.leading = list(range(row_bits - 1, LOW_BITS - 1, -1))
         self.moved = [entry[1] for entry in plan[:-1]]
-        self.packed = self.moved + [[bit for bit in self.leading if bit != self.moved[-1]][0]]
+        self.packed = self.moved + [None]
         self.entries = {}
+        self.table_rows = 0
         for level, packed in enumerate(self.packed):
             free = self.free(level)
             for one in combos(free):
                 for branch in range(2 if level < len(self.moved) else 1):
-                    self.entries[level, pick(one, free), branch] = len(self.entries)
+                    self.entries[level, pick(one, free), branch] = self.table_rows
+                    self.table_rows += BLOCK if packed is None else 2 * BLOCK
 
     def free(self, level):
         return [bit for bit in self.leading if bit != self.packed[level]]
 
     def place(self, level, one, branch=0):
-        first = self.entries[level, pick(one, self.free(level)), branch] * 2 * BLOCK
+        first = self.entries[level, pick(one, self.free(level)), branch]
         return slice(first, first + BLOCK), slice(first + BLOCK, first + 2 * BLOCK)
 
     def row(self, assignment):
@@ -253,7 +255,8 @@
             if level == len(plan) - 1:
                 radius = root(square[0] * (k[0] * k[0]) + square[1] * (k[1] * k[1]))
                 linear = node[0] * width[0] * k[0] + node[1] * width[1] * k[1]
-                store(level, one, 0, (radius - jnp.floor(radius)) + linear)
+                sine, cosine = sincos((radius - jnp.floor(radius)) + linear)
+                table_ref[layout.place(level, one)[0], :] = jnp.where(lanes < 64, cosine, sine)
                 continue
             other = 1 - dimension
             fixed = square[other] * (k[other] * k[other])
@@ -300,22 +303,27 @@
         )
         next_state = {}
         groups = combos(order)
-        step = max(1, len(groups) // DOTS)
+        step = max(1, len(groups) // (DOTS if packed is not None else 8))
         for start in range(0, len(groups), step):
             parts = []
             places = []
             for group in groups[start : start + step]:
                 halves = []
-                for half in range(2):
+                for half in range(1 if packed is None else 2):
                     one = {**group, packed: half}
                     real, imaginary = state[pick(one, free)]
                     turned = []
                     for branch in range(2):
                         cosine, sine = (table_ref[place, :] for place in layout.place(level, one, branch))
-                        both = (real * cosine - imaginary * sine, real * sine + imaginary * cosine)
-                        turned.append(jnp.concatenate(both, 0))
+                        turned.append((real * cosine - imaginary * sine, real * sine + imaginary * cosine))
                     halves.append(turned)
-                values = [jnp.concatenate([turned[branch] for turned in halves], 1) for branch in range(2)]
+                if packed is None:
+                    values = [jnp.concatenate([jnp.concatenate(pair, 1) for pair in halves[0]], 0)]
+                else:
+                    values = [
+                        jnp.concatenate([jnp.concatenate(turned[branch], 0) for turned in halves], 1)
+                        for branch in range(2)
+                    ]
                 tops = [value.astype(jnp.bfloat16) for value in values]
                 parts += tops
                 parts += [
@@ -324,37 +332,40 @@
                 ]
                 places += [pick({**group, moved: branch}, next_free) for branch in range(2)]
             product = jnp.dot(jnp.concatenate(parts, 0), matrix, preferred_element_type=jnp.float32)
-            for index, place in enumerate(places):
-                first = (index // 2 * 4 + index % 2) * 2 * BLOCK
+            count = len(values)
+            for index in range(len(parts) // 2):
+                first = (index // count * 2 * count + index % count) * 2 * BLOCK
                 top = product[first : first + 2 * BLOCK]
-                rest = product[first + 4 * BLOCK : first + 6 * BLOCK]
+                rest = product[first + 2 * count * BLOCK : first + 2 * (count + 1) * BLOCK]
                 total = (top[:, 128:] + rest[:, :128]) + top[:, :128]
-                next_state[place] = (total[:BLOCK], total[BLOCK:])
+                pair = total[:BLOCK], total[BLOCK:]
+                if packed is None:
+                    next_state[places[2 * index]], next_state[places[2 * index + 1]] = pair
+                else:
+                    next_state[places[index]] = pair
         state = next_state
 
-    packed, free = layout.packed[last], layout.free(last)
     copies = []
-    for one in combos(free):
-        real, imaginary = state[pick(one, free)]
-        cosine, sine = (table_ref[place, :] for place in layout.place(last, one))
-        outputs = pack(real * cosine + imaginary * sine, imaginary * cosine - real * sine)
-        for value in range(2):
-            first = layout.row({**one, packed: value})
-            done_ref[first : first + BLOCK, :] = outputs[value]
-        if all(one[bit] == 1 for bit in free[2:]):
-            for value in range(2):
-                shared = {bit: one[bit] for bit in free[:2]}
-                piece = pl.ds(layout.row({**shared, packed: value}), BLOCK << len(free) - 2)
-                copy = pltpu.make_async_copy(done_ref.at[piece], out_ref.at[piece], sems.at[len(copies)])
-                copy.start()
-                copies.append(copy)
+    shared, lower = layout.leading[:3], layout.leading[3:]
+    for one in combos(layout.leading):
+        values = state[pick(one, layout.leading)]
+        wave = table_ref[layout.place(last, one)[0], :]
+        turned = pltpu.roll(wave, 64, 1)
+        cosine, sine = jnp.where(low_half, wave, turned), jnp.where(low_half, turned, -wave)
+        first = layout.row(one)
+        done_ref[first : first + BLOCK, :] = values * cosine + pltpu.roll(values, 64, 1) * sine
+        if all(one[bit] == 1 for bit in lower):
+            piece = pl.ds(layout.row({bit: one[bit] for bit in shared}), BLOCK << len(lower))
+            copy = pltpu.make_async_copy(done_ref.at[piece], out_ref.at[piece], sems.at[len(copies)])
+            copy.start()
+            copies.append(copy)
     for copy in copies:
         copy.wait()
 
 
 def rotations(layout):
     vmem = pl.BlockSpec(memory_space=pltpu.VMEM)
-    rows = 2 * BLOCK * len(layout.entries)
+    rows = layout.table_rows
     return pl.pallas_call(
         functools.partial(table_kernel, layout, ("outer", "inner")),
         out_shape=jax.ShapeDtypeStruct((rows, 128), jnp.float32),

time: 20.3 us -> 20.3 us (level)
  transfers between devices with their start and end apart: 1 -> 1, of which waited for: 1 -> 1; matrix products, arithmetic and copies ran while one was open for 0% -> 0% of each run, Pallas kernels for 8% -> 9%
where the time goes in v6:
time: 20.3 us; the launch traced here: 20 us
  waiting for transfers between devices  8.43 us (42%)
  starting transfers between devices  7.3 us (36%)
  Pallas kernels  3.6 us (18%)
  local copies, waits for them, and re-layouts  0.69 us (3%)
    all_to_all x1, waiting for transfers between devices, body(): rows = lax.all_to_all(weights, ('inner', 'outer'), 0, 0, tiled=True)  8.43 us
    all_to_all x1, starting transfers between devices, body(): rows = lax.all_to_all(weights, ('inner', 'outer'), 0, 0, tiled=True)  7.3 us
    pallas_call x1, Pallas kernels, rotations(): pl.pallas_call(functools.partial(table_kernel, layout, ('outer', 'inner')...  1.83 us
    pallas_call x1, Pallas kernels, run_levels(): pl.pallas_call(functools.partial(level_kernel, layout), out_shape=jax.Sha...  1.78 us
    unnamed x4, local copies, waits for them, and re-layouts  0.69 us
  transfers between devices with their start and end apart: 1, of which 1 were waited for; matrix products, arithmetic and copies ran while one was open for 0% of the time, Pallas kernels for 9%

profile of v6, /device:TPU:0, one launch (start us, length us, event | category | flops | bytes accessed | tf_op | source)
XLA Modules:
  0.0 20.0 jit_solution(2751349892735067995)
XLA Ops:
  0.0 0.0 copy-start
  0.0 7.3 %all-to-all-start = ((f32[32,16,128]{2,1,0:T(8,128)}), f32[32,16,128]{2,1,0:T(8,128)S(1)}, u32[]{:S(2)}, u32[]{:S(2)}) async-start(f32[32,16,128]{2,1,0:T(8,128)} %bitcast.3), calls=%async_computation | async-start | bytes 524288 | tf_op jit(solution)/shard_map/all_to_all | solution.py:429
  7.3 0.0 copy-start.1
  7.3 0.7 %copy-done.1 = f32[8,128]{1,0:T(8,128)S(1)} copy-done((f32[8,128]{1,0:T(8,128)S(1)}, f32[8,128]{1,0:T(8,128)}, u32[]{:S(2)}) %copy-start.1) | copy-done | bytes 4120
  8.0 1.8 %shard_map.37.table_ref = f32[5632,128]{1,0:T(8,128)S(1)} custom-call(f32[8,128]{1,0:T(8,128)S(1)} %copy-done.1), custom_call_target="tpu_custom_call" | custom-call | flops 14417920 | bytes 2883584 | tf_op jit(solution)/shard_map/pallas_call | solution.py:369
  9.8 8.4 %all-to-all-done = f32[32,16,128]{2,1,0:T(8,128)S(1)} async-done(((f32[32,16,128]{2,1,0:T(8,128)}), f32[32,16,128]{2,1,0:T(8,128)S(1)}, u32[]{:S(2)}, u32[]{:S(2)}) %all-to-all-start) | async-done | bytes 262176 | tf_op jit(solution)/shard_map/all_to_all | solution.py:429
  18.3 0.0 copy-done
  18.3 1.8 %shard_map.38 = f32[512,128]{1,0:T(8,128)} custom-call(f32[512,128]{1,0:T(8,128)S(1)} %bitcast.2, f32[5632,128]{1,0:T(8,128)S(1)} %shard_map.37.table_ref, bf16[2,256,256]{2,1,0:T(8,128)(2,1)S(1)} %copy-done), custom_call_target="tpu_custom_call" | custom-call | tf_op jit(solution)/shard_map/pallas_call | solution.py:383
Async XLA Ops:
  0.0 18.3 %copy-start = (bf16[2,256,256]{2,1,0:T(8,128)(2,1)S(1)}, bf16[2,256,256]{2,1,0:T(8,128)(2,1)}, u32[]{:S(2)}) copy-start(bf16[2,256,256]{2,1,0:T(8,128)(2,1)} %constant.5.clone.matrix_ref) | copy-start | bytes 786436
  0.0 18.3 %all-to-all-start = ((f32[32,16,128]{2,1,0:T(8,128)}), f32[32,16,128]{2,1,0:T(8,128)S(1)}, u32[]{:S(2)}, u32[]{:S(2)}) async-start(f32[32,16,128]{2,1,0:T(8,128)} %bitcast.3), calls=%async_computation | async-start | bytes 524288 | tf_op jit(solution)/shard_map/all_to_all | solution.py:429
  7.3 0.7 %copy-start.1 = (f32[8,128]{1,0:T(8,128)S(1)}, f32[8,128]{1,0:T(8,128)}, u32[]{:S(2)}) copy-start(f32[8,128]{1,0:T(8,128)} %constant.4.clone.node_ref) | copy-start | bytes 12292

commit v7 on v5

--- a/solution.py
+++ b/solution.py
@@ -276,10 +276,8 @@
     last = len(layout.moved)
 
     def pack(first, second):
-        return (
-            jnp.where(low_half, first, pltpu.roll(second, 64, 1)),
-            jnp.where(low_half, pltpu.roll(first, 64, 1), second),
-        )
+        crossed = pltpu.roll(jnp.where(low_half, second, first), 64, 1)
+        return jnp.where(low_half, first, crossed), jnp.where(low_half, crossed, second)
 
     state = {}
     for one in combos(layout.free(0)):

time: 20.3 us -> 20.3 us (level)
  no operation moved by 1% of the time
where the time goes in v7:
time: 20.3 us; the launch traced here: 20.1 us
  waiting for transfers between devices  8.58 us (42%)
  starting transfers between devices  7.3 us (36%)
  Pallas kernels  3.47 us (17%)
  local copies, waits for them, and re-layouts  0.69 us (3%)
    all_to_all x1, waiting for transfers between devices, body(): rows = lax.all_to_all(weights, ('inner', 'outer'), 0, 0, tiled=True)  8.58 us
    all_to_all x1, starting transfers between devices, body(): rows = lax.all_to_all(weights, ('inner', 'outer'), 0, 0, tiled=True)  7.3 us
    pallas_call x1, Pallas kernels, run_levels(): pl.pallas_call(functools.partial(level_kernel, layout), out_shape=jax.Sha...  1.79 us
    pallas_call x1, Pallas kernels, rotations(): pl.pallas_call(functools.partial(table_kernel, layout, ('outer', 'inner')...  1.68 us
    unnamed x4, local copies, waits for them, and re-layouts  0.69 us
  transfers between devices with their start and end apart: 1, of which 1 were waited for; matrix products, arithmetic and copies ran while one was open for 0% of the time, Pallas kernels for 8%

profile of v7, /device:TPU:0, one launch (start us, length us, event | category | flops | bytes accessed | tf_op | source)
XLA Modules:
  0.0 20.1 jit_solution(18011605341451730831)
XLA Ops:
  0.0 0.0 copy-start
  0.0 7.3 %all-to-all-start = ((f32[32,16,128]{2,1,0:T(8,128)}), f32[32,16,128]{2,1,0:T(8,128)S(1)}, u32[]{:S(2)}, u32[]{:S(2)}) async-start(f32[32,16,128]{2,1,0:T(8,128)} %bitcast.3), calls=%async_computation | async-start | bytes 524288 | tf_op jit(solution)/shard_map/all_to_all | solution.py:416
  7.3 0.0 copy-start.1
  7.3 0.7 %copy-done.1 = f32[8,128]{1,0:T(8,128)S(1)} copy-done((f32[8,128]{1,0:T(8,128)S(1)}, f32[8,128]{1,0:T(8,128)}, u32[]{:S(2)}) %copy-start.1) | copy-done | bytes 4120
  8.0 1.7 %shard_map.37.table_ref = f32[5632,128]{1,0:T(8,128)S(1)} custom-call(f32[8,128]{1,0:T(8,128)S(1)} %copy-done.1), custom_call_target="tpu_custom_call" | custom-call | flops 14417920 | bytes 2883584 | tf_op jit(solution)/shard_map/pallas_call | solution.py:356
  9.7 8.6 %all-to-all-done = f32[32,16,128]{2,1,0:T(8,128)S(1)} async-done(((f32[32,16,128]{2,1,0:T(8,128)}), f32[32,16,128]{2,1,0:T(8,128)S(1)}, u32[]{:S(2)}, u32[]{:S(2)}) %all-to-all-start) | async-done | bytes 262176 | tf_op jit(solution)/shard_map/all_to_all | solution.py:416
  18.3 0.0 copy-done
  18.3 1.8 %shard_map.38 = f32[512,128]{1,0:T(8,128)} custom-call(f32[512,128]{1,0:T(8,128)S(1)} %bitcast.2, f32[5632,128]{1,0:T(8,128)S(1)} %shard_map.37.table_ref, bf16[2,256,256]{2,1,0:T(8,128)(2,1)S(1)} %copy-done), custom_call_target="tpu_custom_call" | custom-call | tf_op jit(solution)/shard_map/pallas_call | solution.py:370
Async XLA Ops:
  0.0 18.3 %copy-start = (bf16[2,256,256]{2,1,0:T(8,128)(2,1)S(1)}, bf16[2,256,256]{2,1,0:T(8,128)(2,1)}, u32[]{:S(2)}) copy-start(bf16[2,256,256]{2,1,0:T(8,128)(2,1)} %constant.5.clone.matrix_ref) | copy-start | bytes 786436
  0.0 18.3 %all-to-all-start = ((f32[32,16,128]{2,1,0:T(8,128)}), f32[32,16,128]{2,1,0:T(8,128)S(1)}, u32[]{:S(2)}, u32[]{:S(2)}) async-start(f32[32,16,128]{2,1,0:T(8,128)} %bitcast.3), calls=%async_computation | async-start | bytes 524288 | tf_op jit(solution)/shard_map/all_to_all | solution.py:416
  7.3 0.7 %copy-start.1 = (f32[8,128]{1,0:T(8,128)S(1)}, f32[8,128]{1,0:T(8,128)}, u32[]{:S(2)}) copy-start(f32[8,128]{1,0:T(8,128)} %constant.4.clone.node_ref) | copy-start | bytes 12292

commit v8 on v7

--- a/solution.py
+++ b/solution.py
@@ -13,7 +13,7 @@
 LOW_BITS = 3
 BLOCK = 1 << LOW_BITS
 VMEM_BYTES = 16 * 1024 * 1024
-DOTS = 4
+DOTS = 2
 
 
 def chebyshev_nodes():
@@ -300,7 +300,7 @@
         groups = combos(order)
         step = max(1, len(groups) // DOTS)
         for start in range(0, len(groups), step):
-            parts = []
+            parts = [[], []]
             places = []
             for group in groups[start : start + step]:
                 halves = []
@@ -315,18 +315,18 @@
                     halves.append(turned)
                 values = [jnp.concatenate([turned[branch] for turned in halves], 1) for branch in range(2)]
                 tops = [value.astype(jnp.bfloat16) for value in values]
-                parts += tops
-                parts += [
-                    (value - top.astype(jnp.float32)).astype(jnp.bfloat16)
+                parts[0] += tops
+                parts[1] += [
+                    (value - top.astype(jnp.float32))
                     for value, top in zip(values, tops)
                 ]
                 places += [pick({**group, moved: branch}, next_free) for branch in range(2)]
-            product = jnp.dot(jnp.concatenate(parts, 0), matrix, preferred_element_type=jnp.float32)
+            tops = jnp.dot(jnp.concatenate(parts[0], 0), matrix, preferred_element_type=jnp.float32)
+            rests = jnp.dot(jnp.concatenate(parts[1], 0), matrix[:, :128].astype(jnp.float32), preferred_element_type=jnp.float32)
             for index, place in enumerate(places):
-                first = (index // 2 * 4 + index % 2) * 2 * BLOCK
-                top = product[first : first + 2 * BLOCK]
-                rest = product[first + 4 * BLOCK : first + 6 * BLOCK]
-                total = (top[:, 128:] + rest[:, :128]) + top[:, :128]
+                first = index * 2 * BLOCK
+                top, rest = tops[first : first + 2 * BLOCK], rests[first : first + 2 * BLOCK]
+                total = (top[:, 128:] + rest) + top[:, :128]
                 next_state[place] = (total[:BLOCK], total[BLOCK:])
         state = next_state
 

time: 20.3 us -> 20.3 us (level)
  no operation moved by 1% of the time
where the time goes in v8:
time: 20.3 us; the launch traced here: 20 us
  waiting for transfers between devices  8.58 us (42%)
  starting transfers between devices  7.3 us (36%)
  Pallas kernels  3.44 us (17%)
  local copies, waits for them, and re-layouts  0.69 us (3%)
    all_to_all x1, waiting for transfers between devices, body(): rows = lax.all_to_all(weights, ('inner', 'outer'), 0, 0, tiled=True)  8.58 us
    all_to_all x1, starting transfers between devices, body(): rows = lax.all_to_all(weights, ('inner', 'outer'), 0, 0, tiled=True)  7.3 us
    pallas_call x1, Pallas kernels, run_levels(): pl.pallas_call(functools.partial(level_kernel, layout), out_shape=jax.Sha...  1.76 us
    pallas_call x1, Pallas kernels, rotations(): pl.pallas_call(functools.partial(table_kernel, layout, ('outer', 'inner')...  1.68 us
    unnamed x4, local copies, waits for them, and re-layouts  0.69 us
  transfers between devices with their start and end apart: 1, of which 1 were waited for; matrix products, arithmetic and copies ran while one was open for 0% of the time, Pallas kernels for 8%

profile of v8, /device:TPU:0, one launch (start us, length us, event | category | flops | bytes accessed | tf_op | source)
XLA Modules:
  0.0 20.0 jit_solution(8233846864763793282)
XLA Ops:
  0.0 0.0 copy-start
  0.0 7.3 %all-to-all-start = ((f32[32,16,128]{2,1,0:T(8,128)}), f32[32,16,128]{2,1,0:T(8,128)S(1)}, u32[]{:S(2)}, u32[]{:S(2)}) async-start(f32[32,16,128]{2,1,0:T(8,128)} %bitcast.3), calls=%async_computation | async-start | bytes 524288 | tf_op jit(solution)/shard_map/all_to_all | solution.py:416
  7.3 0.0 copy-start.1
  7.3 0.7 %copy-done.1 = f32[8,128]{1,0:T(8,128)S(1)} copy-done((f32[8,128]{1,0:T(8,128)S(1)}, f32[8,128]{1,0:T(8,128)}, u32[]{:S(2)}) %copy-start.1) | copy-done | bytes 4120
  8.0 1.7 %shard_map.37.table_ref = f32[5632,128]{1,0:T(8,128)S(1)} custom-call(f32[8,128]{1,0:T(8,128)S(1)} %copy-done.1), custom_call_target="tpu_custom_call" | custom-call | flops 14417920 | bytes 2883584 | tf_op jit(solution)/shard_map/pallas_call | solution.py:356
  9.7 8.6 %all-to-all-done = f32[32,16,128]{2,1,0:T(8,128)S(1)} async-done(((f32[32,16,128]{2,1,0:T(8,128)}), f32[32,16,128]{2,1,0:T(8,128)S(1)}, u32[]{:S(2)}, u32[]{:S(2)}) %all-to-all-start) | async-done | bytes 262176 | tf_op jit(solution)/shard_map/all_to_all | solution.py:416
  18.3 0.0 copy-done
  18.3 1.8 %shard_map.38 = f32[512,128]{1,0:T(8,128)} custom-call(f32[512,128]{1,0:T(8,128)S(1)} %bitcast.2, f32[5632,128]{1,0:T(8,128)S(1)} %shard_map.37.table_ref, bf16[2,256,256]{2,1,0:T(8,128)(2,1)S(1)} %copy-done), custom_call_target="tpu_custom_call" | custom-call | tf_op jit(solution)/shard_map/pallas_call | solution.py:370
Async XLA Ops:
  0.0 18.3 %copy-start = (bf16[2,256,256]{2,1,0:T(8,128)(2,1)S(1)}, bf16[2,256,256]{2,1,0:T(8,128)(2,1)}, u32[]{:S(2)}) copy-start(bf16[2,256,256]{2,1,0:T(8,128)(2,1)} %constant.5.clone.matrix_ref) | copy-start | bytes 786436
  0.0 18.3 %all-to-all-start = ((f32[32,16,128]{2,1,0:T(8,128)}), f32[32,16,128]{2,1,0:T(8,128)S(1)}, u32[]{:S(2)}, u32[]{:S(2)}) async-start(f32[32,16,128]{2,1,0:T(8,128)} %bitcast.3), calls=%async_computation | async-start | bytes 524288 | tf_op jit(solution)/shard_map/all_to_all | solution.py:416
  7.3 0.7 %copy-start.1 = (f32[8,128]{1,0:T(8,128)S(1)}, f32[8,128]{1,0:T(8,128)}, u32[]{:S(2)}) copy-start(f32[8,128]{1,0:T(8,128)} %constant.4.clone.node_ref) | copy-start | bytes 12292

commit v9 on v8

--- a/solution.py
+++ b/solution.py
@@ -317,12 +317,12 @@
                 tops = [value.astype(jnp.bfloat16) for value in values]
                 parts[0] += tops
                 parts[1] += [
-                    (value - top.astype(jnp.float32))
+                    (value - top.astype(jnp.float32)).astype(jnp.bfloat16)
                     for value, top in zip(values, tops)
                 ]
                 places += [pick({**group, moved: branch}, next_free) for branch in range(2)]
             tops = jnp.dot(jnp.concatenate(parts[0], 0), matrix, preferred_element_type=jnp.float32)
-            rests = jnp.dot(jnp.concatenate(parts[1], 0), matrix[:, :128].astype(jnp.float32), preferred_element_type=jnp.float32)
+            rests = jnp.dot(jnp.concatenate(parts[1], 0), matrix[:, :128], preferred_element_type=jnp.float32)
             for index, place in enumerate(places):
                 first = index * 2 * BLOCK
                 top, rest = tops[first : first + 2 * BLOCK], rests[first : first + 2 * BLOCK]

time: 20.3 us -> 20.3 us (level)
  no operation moved by 1% of the time
where the time goes in v9:
time: 20.3 us; the launch traced here: 20.1 us
  waiting for transfers between devices  8.58 us (42%)
  starting transfers between devices  7.3 us (36%)
  Pallas kernels  3.48 us (17%)
  local copies, waits for them, and re-layouts  0.69 us (3%)
    all_to_all x1, waiting for transfers between devices, body(): rows = lax.all_to_all(weights, ('inner', 'outer'), 0, 0, tiled=True)  8.58 us
    all_to_all x1, starting transfers between devices, body(): rows = lax.all_to_all(weights, ('inner', 'outer'), 0, 0, tiled=True)  7.3 us
    pallas_call x1, Pallas kernels, run_levels(): pl.pallas_call(functools.partial(level_kernel, layout), out_shape=jax.Sha...  1.8 us
    pallas_call x1, Pallas kernels, rotations(): pl.pallas_call(functools.partial(table_kernel, layout, ('outer', 'inner')...  1.68 us
    unnamed x4, local copies, waits for them, and re-layouts  0.69 us
  transfers between devices with their start and end apart: 1, of which 1 were waited for; matrix products, arithmetic and copies ran while one was open for 0% of the time, Pallas kernels for 8%

profile of v9, /device:TPU:0, one launch (start us, length us, event | category | flops | bytes accessed | tf_op | source)
XLA Modules:
  0.0 20.1 jit_solution(14702667692074594634)
XLA Ops:
  0.0 0.0 copy-start
  0.0 7.3 %all-to-all-start = ((f32[32,16,128]{2,1,0:T(8,128)}), f32[32,16,128]{2,1,0:T(8,128)S(1)}, u32[]{:S(2)}, u32[]{:S(2)}) async-start(f32[32,16,128]{2,1,0:T(8,128)} %bitcast.3), calls=%async_computation | async-start | bytes 524288 | tf_op jit(solution)/shard_map/all_to_all | solution.py:416
  7.3 0.0 copy-start.1
  7.3 0.7 %copy-done.1 = f32[8,128]{1,0:T(8,128)S(1)} copy-done((f32[8,128]{1,0:T(8,128)S(1)}, f32[8,128]{1,0:T(8,128)}, u32[]{:S(2)}) %copy-start.1) | copy-done | bytes 4120
  8.0 1.7 %shard_map.37.table_ref = f32[5632,128]{1,0:T(8,128)S(1)} custom-call(f32[8,128]{1,0:T(8,128)S(1)} %copy-done.1), custom_call_target="tpu_custom_call" | custom-call | flops 14417920 | bytes 2883584 | tf_op jit(solution)/shard_map/pallas_call | solution.py:356
  9.7 8.6 %all-to-all-done = f32[32,16,128]{2,1,0:T(8,128)S(1)} async-done(((f32[32,16,128]{2,1,0:T(8,128)}), f32[32,16,128]{2,1,0:T(8,128)S(1)}, u32[]{:S(2)}, u32[]{:S(2)}) %all-to-all-start) | async-done | bytes 262176 | tf_op jit(solution)/shard_map/all_to_all | solution.py:416
  18.3 0.0 copy-done
  18.3 1.8 %shard_map.38 = f32[512,128]{1,0:T(8,128)} custom-call(f32[512,128]{1,0:T(8,128)S(1)} %bitcast.2, f32[5632,128]{1,0:T(8,128)S(1)} %shard_map.37.table_ref, bf16[2,256,256]{2,1,0:T(8,128)(2,1)S(1)} %copy-done), custom_call_target="tpu_custom_call" | custom-call | tf_op jit(solution)/shard_map/pallas_call | solution.py:370
Async XLA Ops:
  0.0 18.3 %copy-start = (bf16[2,256,256]{2,1,0:T(8,128)(2,1)S(1)}, bf16[2,256,256]{2,1,0:T(8,128)(2,1)}, u32[]{:S(2)}) copy-start(bf16[2,256,256]{2,1,0:T(8,128)(2,1)} %constant.5.clone.matrix_ref) | copy-start | bytes 786436
  0.0 18.3 %all-to-all-start = ((f32[32,16,128]{2,1,0:T(8,128)}), f32[32,16,128]{2,1,0:T(8,128)S(1)}, u32[]{:S(2)}, u32[]{:S(2)}) async-start(f32[32,16,128]{2,1,0:T(8,128)} %bitcast.3), calls=%async_computation | async-start | bytes 524288 | tf_op jit(solution)/shard_map/all_to_all | solution.py:416
  7.3 0.7 %copy-start.1 = (f32[8,128]{1,0:T(8,128)S(1)}, f32[8,128]{1,0:T(8,128)}, u32[]{:S(2)}) copy-start(f32[8,128]{1,0:T(8,128)} %constant.4.clone.node_ref) | copy-start | bytes 12292
